TPU v7x, 256 devices: a whole 4x4x8 slice. The times are simulated.
256 devices in a mesh: space: 8 (over z_hi, y), dp: 32 (over x, z_lo, core).
Axes of the slice: x: 4, y: 4, z: 8 (z_hi: 2, z_lo: 4; z = z_hi * 4 + z_lo), core: 2. Of those that a mesh axis runs over, the one named last changes fastest.
Arguments:
- features: bfloat16 [32, 48, 64, 8, 128], P('dp', None, 'space'), may hold values from -21 to 21
- upstream: bfloat16 [32, 48, 64, 8, 128], P('dp', None, 'space'), may hold values from -21 to 21
- weight_one: bfloat16 [48, 48, 3, 3, 3], replicated, may hold values from -0.15625 to 0.15625
- weight_two: bfloat16 [48, 48, 3, 3, 3], replicated, may hold values from -0.15625 to 0.15625
- norm_gain: float32 [48], replicated, may hold values from 0.25 to 1.75
- norm_bias: float32 [48], replicated, may hold values from -3 to 3
Outputs:
- grad_input: bfloat16 [32, 48, 64, 8, 128], P('dp', None, 'space')
- grad_one: float32 [48, 48, 3, 3, 3], replicated
- grad_two: float32 [48, 48, 3, 3, 3], replicated
- grad_gain: float32 [48], replicated
- grad_bias: float32 [48], replicated
All inputs are finite; a program needn't handle non-finite values.
Results may differ from a plain program's by a relative error of at most 0.0029.
Values may be sent and summed in bfloat16 or wider, within the bound.
A program may use at most 128 MiB of HBM per device.

v0:
```python
import jax
import jax.numpy as jnp
from jax import lax
from jax.sharding import PartitionSpec as P

epsilon = 1e-05


def padded_2(cells, sides, width):
    for axis, dim in sides:
        count = lax.axis_size(axis)
        ends = count - 1
        head = lax.slice_in_dim(cells, 0, width, axis=dim)
        tail = lax.slice_in_dim(cells, cells.shape[dim] - width, cells.shape[dim], axis=dim)
        cells = jnp.concatenate(
            [
                lax.ppermute(tail, axis, [(i, (i + 1) % count) for i in range(ends)]),
                cells,
                lax.ppermute(head, axis, [((i + 1) % count, i) for i in range(ends)]),
            ],
            axis=dim,
        )
    return cells


def slab_faces(field):
    return padded_2(field, (("space", 2),), 1)


def conv_slab(padded, kernel):
    return lax.conv_general_dilated(
        padded,
        kernel,
        (1, 1, 1),
        ((0, 0), (1, 1), (1, 1)),
        dimension_numbers=("NCDHW", "OIDHW", "NCDHW"),
        preferred_element_type=jnp.float32,
    )


def flipped(kernel):
    return jnp.transpose(kernel, (1, 0, 2, 3, 4))[:, :, ::-1, ::-1, ::-1]


def kernel_grad(padded, target):
    return lax.conv_general_dilated(
        padded,
        target,
        (1, 1, 1),
        ((0, 0), (1, 1), (1, 1)),
        dimension_numbers=("CNDHW", "IODHW", "CNDHW"),
        preferred_element_type=jnp.float32,
    )


def local(features, upstream, weight_one, weight_two, norm_gain, norm_bias):
    axes_cells = (2, 3, 4)
    cells_all = float(
        features.shape[2] * features.shape[3] * features.shape[4] * lax.axis_size("space")
    )
    padded_x = slab_faces(features)
    pre_act = conv_slab(padded_x, weight_one)
    sums_pre, squares_pre = lax.psum(
        (
            jnp.sum(pre_act, axis=axes_cells, keepdims=True),
            jnp.sum(pre_act * pre_act, axis=axes_cells, keepdims=True),
        ),
        "space",
    )
    mean_pre = sums_pre / cells_all
    inv_std = lax.rsqrt(squares_pre / cells_all - mean_pre * mean_pre + epsilon)
    normal_hat = (pre_act - mean_pre) * inv_std
    gain_b = norm_gain.reshape(1, -1, 1, 1, 1)
    normed = normal_hat * gain_b + norm_bias.reshape(1, -1, 1, 1, 1)
    sigmoid_val = jax.nn.sigmoid(normed)
    hidden = (normed * sigmoid_val).astype(jnp.bfloat16)
    padded_h = slab_faces(hidden)
    padded_g = slab_faces(upstream)
    local_two = kernel_grad(padded_h, upstream)
    grad_hidden = conv_slab(padded_g, flipped(weight_two))
    grad_norm = grad_hidden * sigmoid_val * (1.0 + normed * (1.0 - sigmoid_val))
    local_bias = jnp.sum(grad_norm, axis=(0, 2, 3, 4))
    local_gain = jnp.sum(grad_norm * normal_hat, axis=(0, 2, 3, 4))
    slope_sum, slope_dot = lax.psum(
        (
            jnp.sum(grad_norm, axis=axes_cells, keepdims=True),
            jnp.sum(grad_norm * normal_hat, axis=axes_cells, keepdims=True),
        ),
        "space",
    )
    grad_pre = (
        gain_b
        * inv_std
        * (grad_norm - slope_sum / cells_all - normal_hat * (slope_dot / cells_all))
    ).astype(jnp.bfloat16)
    padded_grad = slab_faces(grad_pre)
    local_one = kernel_grad(padded_x, grad_pre)
    back = conv_slab(padded_grad, flipped(weight_one))
    grad_input = (upstream.astype(jnp.float32) + back).astype(jnp.bfloat16)
    grad_one, grad_two, grad_gain, grad_bias = lax.psum(
        (local_one, local_two, local_gain, local_bias), ("space", "dp")
    )
    return (grad_input, grad_one, grad_two, grad_gain, grad_bias)


def solution(mesh):
    in_specs = (
        P("dp", None, "space", None, None),
        P("dp", None, "space", None, None),
        P(),
        P(),
        P(),
        P(),
    )
    out_specs = (P("dp", None, "space", None, None), P(), P(), P(), P())
    return jax.shard_map(local, mesh=mesh, in_specs=in_specs, out_specs=out_specs, check_vma=False)
```

profile of v0, /device:TPU:1, one launch (start us, length us, event | category | flops | bytes accessed | tf_op | source)
XLA Modules:
  0.0 684.3 jit_solution(1534281291638809892)
XLA Ops:
  7.2 1.0 fusion.73
  8.3 4.2 collective-permute-start
  12.5 1.3 collective-permute-start.1
  13.8 1.6 fusion.74
  15.4 4.6 collective-permute-start.2
  20.0 1.3 collective-permute-start.3
  21.3 7.4 %copy.112 = bf16[1,48,8,8,128]{1,0,4,3,2:T(2,128)(2,1)} copy(bf16[1,48,8,8,128]{4,3,2,1,0:T(8,128)(2,1)} %param.7) | data formatting | bytes 1572864 | tf_op args[1]
  28.7 2.5 copy.85
  31.3 3.5 copy.86
  34.8 3.6 fusion.70
  38.4 3.1 fusion.68
  42.1 1.5 copy-done.10
  43.6 0.8 slice.50
  44.4 2.0 pad_maximum_fusion.3
  46.5 4.9 copy.89
  51.3 2.3 pad.2
  53.7 0.5 copy.91
  54.2 0.8 slice.51
  55.0 1.2 copy-done.11
  56.6 12.1 %select_reduce_fusion.3 = (f32[48]{0:T(128)S(1)}, f32[48]{0:T(128)S(1)}, f32[8,8,8,17,48]{4,2,3,1,0:T(8,128)}) fusion(pred[8,17]{0,1:T(8,128)(4,1)S(1)} %copy-done.14, bf16[48,48,3,3,3]{1,0,4,3,2:T(8,128)(2,1)S(1)} %copy-done, bf16[48,10,8,1,7,2]{0,4,5,2,1,3:T(8,128)(2,1)S(1)} %copy-done.13, bf16[48,10,8,1,8,17]{0,4,5,2,1,3:T(8,128)(2,1)S(1)} %copy-done.11), kind=kOutput, calls=%fused_computation.25 | convolution fusion | flops 998682496 | bytes 2948104 | tf_op jit(solution)/shard_map/conv_general_dilated | solution.py:31
  68.7 30.8 %all-reduce.3 = (f32[1,48,1,1,1]{1,4,3,2,0:T(1,128)S(1)}, f32[1,48,1,1,1]{1,4,3,2,0:T(1,128)S(1)}) all-reduce(f32[1,48,1,1,1]{1,4,3,2,0:T(1,128)S(1)} %bitcast.113, f32[1,48,1,1,1]{1,4,3,2,0:T(1,128)S(1)} %bitcast.112), channel_id=1, replica_groups=mesh['space'=8,'dp'=32] {'space'}, use_global_device_ids=true, to_apply=%region_1.0 | all-reduce | flops 96 | bytes 768 | tf_op jit(solution)/shard_map/psum | solution.py:63
  99.5 16.4 %select_reduce_fusion = (f32[48]{0:T(128)S(1)}, f32[48]{0:T(128)S(1)}, f32[8,8,8,17,48]{4,2,3,1,0:T(8,128)}) fusion(pred[8,17]{0,1:T(8,128)(4,1)S(1)} %copy-done.14, f32[48]{0:T(128)S(1)} %bitcast.108, f32[48]{0:T(128)S(1)} %get-tuple-element.55, f32[8,8,8,17,48]{4,2,3,1,0:T(8,128)} %get-tuple-element.56, f32[48]{0:T(128)S(1)} %copy-done.16, ...), kind=kOutput, calls=%fused_computation.17 | convolution fusion | flops 1004113792 | bytes 4620040 | tf_op jit(solution)/shard_map/conv_general_dilated | solution.py:31
  115.9 25.0 %all-reduce.2 = (f32[1,48,1,1,1]{1,4,3,2,0:T(1,128)S(1)}, f32[1,48,1,1,1]{1,4,3,2,0:T(1,128)S(1)}) all-reduce(f32[1,48,1,1,1]{1,4,3,2,0:T(1,128)S(1)} %bitcast.111, f32[1,48,1,1,1]{1,4,3,2,0:T(1,128)S(1)} %bitcast.110), channel_id=1, replica_groups=mesh['space'=8,'dp'=32] {'space'}, use_global_device_ids=true, to_apply=%region_5.0 | all-reduce | flops 96 | bytes 768 | tf_op jit(solution)/shard_map/psum | solution.py:84
  140.9 4.9 multiply_convert_fusion.1
  146.3 1.2 copy.128
  147.5 2.2 collective-permute-start.6
  149.8 1.2 copy.127
  151.0 1.3 collective-permute-start.7
  152.3 2.3 copy.117
  154.6 2.3 copy.118
  156.9 1.9 copy.104
  159.0 4.0 collective-permute-start.4
  163.0 1.3 collective-permute-start.5
  164.3 1.5 fusion.36
  165.9 17.9 %fusion.49 = f32[48,48,3,3,3]{0,1,4,3,2:T(8,128)} fusion(bf16[8,8,8,17,48]{4,2,3,1,0:T(8,128)(2,1)S(1)} %get-tuple-element.40, pred[8,17]{0,1:T(8,128)(4,1)S(1)} %copy-done.14, bf16[48,10,8,8,17,1]{0,3,5,4,2,1:T(8,128)(2,1)S(1)} %get-tuple-element.60, bf16[48,10,8,8,17,1]{0,3,5,4,2,1:T(8,128)(2,1)} %copy.104, ...), kind=kOutput, calls=%fused_computation.61 | convolution fusion | flops 1002491904 | bytes 4217992 | tf_op jit(solution)/shard_map/conv_general_dilated | solution.py:46
  184.3 6.4 copy.126
  190.7 101.2 %all-reduce = (f32[48]{0:T(128)}, f32[48]{0:T(128)}) all-reduce(f32[48]{0:T(128)S(1)} %get-tuple-element.25, f32[48]{0:T(128)S(1)} %get-tuple-element.26), channel_id=1, replica_groups=mesh['space'=8,'dp'=32] {'space','dp'}, use_global_device_ids=true, to_apply=%region_10.0 | all-reduce | flops 96 | bytes 768 | tf_op jit(solution)/shard_map/psum | solution.py:100
  291.9 0.6 maximum_bitcast_fusion
  292.5 0.6 pad.7
  293.7 10.5 %broadcast_select_fusion = f32[8,8,8,17,48]{4,2,3,1,0:T(8,128)S(1)} fusion(pred[8,17]{0,1:T(8,128)(4,1)S(1)} %copy-done.14, bf16[48,48,3,3,3]{1,0,4,3,2:T(8,128)(2,1)S(1)} %copy-done, bf16[48,10,8,1,7,2]{0,4,5,2,1,3:T(8,128)(2,1)S(1)} %slice.57, bf16[48,10,8,1,8,17]{0,4,5,2,1,3:T(8,128)(2,1)S(1)} %copy.98), kind=kOutput, calls=%fused_computation.55 | convolution fusion | flops 996593664 | bytes 2947720 | tf_op jit(solution)/shard_map/conv_general_dilated | solution.py:31
  304.2 3.1 copy.99
  307.4 1.8 copy-done.8
  309.3 110.6 %fusion.11 = f32[48,48,3,3,3]{0,1,4,3,2:T(8,128)} fusion(bf16[1,48,8,8,128]{1,0,4,3,2:T(2,128)(2,1)S(1)} %copy-done.7, bf16[1,48,1,8,128]{1,0,4,3,2:T(2,128)(2,1)} %collective-permute-done.7, bf16[1,48,8,8,128]{1,0,4,3,2:T(2,128)(2,1)S(1)} %bitcast.102, bf16[1,48,1,8,128]{1,0,4,3,2:T(2,128)(2,1)} %collective-permute-done.6), kind=kOutput, calls=%fused_computation.15 | convolution fusion | flops 932364288 | bytes 2018304 | tf_op jit(solution)/shard_map/conv_general_dilated | solution.py:46
  419.9 4.1 fusion.13
  424.0 3.8 copy.113
  427.8 245.1 %all-reduce.6.cloned.1.call-done = (f32[48,48,3,3,3]{0,1,4,3,2:T(8,128)}, f32[48,48,3,3,3]{0,1,4,3,2:T(8,128)}) async-done(((f32[48,48,3,3,3]{0,1,4,3,2:T(8,128)}, f32[48,48,3,3,3]{0,1,4,3,2:T(8,128)}), (f32[48,48,3,3,3]{0,1,4,3,2:T(8,128)}, f32[48,48,3,3,3]{0,1,4,3,2:T(8,128)})) %all-reduce.6.cloned.1.call-update) | async-done | bytes 497680 | tf_op jit(solution)/shard_map/psum | solution.py:100
  672.9 2.2 copy.114
  675.1 2.2 copy.115
  (64 shorter events, 3.1 us)
Async XLA Ops:
  7.2 47.9 %copy-start = (bf16[48,48,3,3,3]{1,0,4,3,2:T(8,128)(2,1)S(1)}, bf16[48,48,3,3,3]{1,0,4,3,2:T(8,128)(2,1)}, u32[]{:S(2)}) copy-start(bf16[48,48,3,3,3]{1,0,4,3,2:T(8,128)(2,1)} %param.8) | copy-start | bytes 373252
  7.2 21.5 %copy-start.5 = (bf16[1,48,8,8,128]{4,3,2,1,0:T(8,128)(2,1)S(1)}, bf16[1,48,8,8,128]{4,3,2,1,0:T(8,128)(2,1)}, u32[]{:S(2)}) copy-start(bf16[1,48,8,8,128]{4,3,2,1,0:T(8,128)(2,1)} %param.7) | copy-start | bytes 2359300
  7.2 665.7 %all-reduce.6.cloned.1.call-start = ((), (), s32[]{:S(2)}) async-start(), calls=%async_computation | async-start | bytes 2654208 | tf_op jit(solution)/shard_map/psum | solution.py:100
  8.3 22.9 %copy-start.12 = (bf16[1,48,8,8,128]{4,3,2,1,0:T(8,128)(2,1)S(1)}, bf16[1,48,8,8,128]{4,3,2,1,0:T(8,128)(2,1)}, u32[]{:S(2)}) copy-start(bf16[1,48,8,8,128]{4,3,2,1,0:T(8,128)(2,1)} %param.6) | copy-start | bytes 2359300
  8.3 22.9 %collective-permute-start = (bf16[1,48,1,8,128]{4,3,2,1,0:T(8,128)(2,1)S(1)}, bf16[1,48,1,8,128]{4,3,2,1,0:T(8,128)(2,1)S(1)}, u32[]{:S(2)}, u32[]{:S(2)}) collective-permute-start(bf16[1,48,1,8,128]{4,3,2,1,0:T(8,128)(2,1)S(1)} %get-tuple-element.51), channel_id=1, source_target_pairs={{0,32},{32,64},{64,96},{96,128},{128,160},{160,192},{192,224},{1,3... | collective-permute-start | bytes 294920 | tf_op jit(solution)/shard_map/ppermute | solution.py:17
  12.5 18.7 %collective-permute-start.1 = (bf16[1,48,1,8,128]{4,3,2,1,0:T(8,128)(2,1)S(1)}, bf16[1,48,1,8,128]{4,3,2,1,0:T(8,128)(2,1)S(1)}, u32[]{:S(2)}, u32[]{:S(2)}) collective-permute-start(bf16[1,48,1,8,128]{4,3,2,1,0:T(8,128)(2,1)S(1)} %get-tuple-element.52), channel_id=1, source_target_pairs={{32,0},{64,32},{96,64},{128,96},{160,128},{192,160},{224,192},{33,... | collective-permute-start | bytes 294920 | tf_op jit(solution)/shard_map/ppermute | solution.py:19
  15.4 29.1 %collective-permute-start.2 = (bf16[1,48,1,8,128]{4,3,2,1,0:T(8,128)(2,1)}, bf16[1,48,1,8,128]{4,3,2,1,0:T(8,128)(2,1)}, u32[]{:S(2)}, u32[]{:S(2)}) collective-permute-start(bf16[1,48,1,8,128]{4,3,2,1,0:T(8,128)(2,1)} %get-tuple-element.53), channel_id=1, source_target_pairs={{0,32},{32,64},{64,96},{96,128},{128,160},{160,192},{192,224},{1,3... | collective-permute-start | bytes 294920 | tf_op jit(solution)/shard_map/ppermute | solution.py:17
  20.0 24.4 %collective-permute-start.3 = (bf16[1,48,1,8,128]{4,3,2,1,0:T(8,128)(2,1)S(1)}, bf16[1,48,1,8,128]{4,3,2,1,0:T(8,128)(2,1)}, u32[]{:S(2)}, u32[]{:S(2)}) collective-permute-start(bf16[1,48,1,8,128]{4,3,2,1,0:T(8,128)(2,1)S(1)} %get-tuple-element.54), channel_id=1, source_target_pairs={{32,0},{64,32},{96,64},{128,96},{160,128},{192,160},{224,192},{33,... | collective-permute-start | bytes 294920 | tf_op jit(solution)/shard_map/ppermute | solution.py:19
  41.5 2.9 copy-start.6
  42.1 1.6 copy-start.10
  53.7 2.6 copy-start.11
  53.7 2.8 copy-start.13
  53.7 2.8 copy-start.14
  54.2 14.5 %copy-start.9 = (bf16[48,10,8,1,8,17]{0,4,5,2,1,3:T(8,128)(2,1)}, bf16[48,10,8,1,8,17]{0,4,5,2,1,3:T(8,128)(2,1)S(1)}, u32[]{:S(2)}) copy-start(bf16[48,10,8,1,8,17]{0,4,5,2,1,3:T(8,128)(2,1)S(1)} %copy.91) | copy-start | bytes 3133444
  56.5 43.0 %copy-start.15 = (f32[48]{0:T(128)S(1)}, f32[48]{0:T(128)}, u32[]{:S(2)}) copy-start(f32[48]{0:T(128)} %param.10) | copy-start | bytes 580
  56.5 43.0 %copy-start.16 = (f32[48]{0:T(128)S(1)}, f32[48]{0:T(128)}, u32[]{:S(2)}) copy-start(f32[48]{0:T(128)} %param.11) | copy-start | bytes 580
  145.8 6.5 copy-start.3
  146.2 8.3 %copy-start.2 = (bf16[48,10,8,1,8,16]{0,2,5,4,1,3:T(8,128)(2,1)S(1)}, bf16[48,10,8,1,8,16]{0,2,5,4,1,3:T(8,128)(2,1)}, u32[]{:S(2)}) copy-start(bf16[48,10,8,1,8,16]{0,2,5,4,1,3:T(8,128)(2,1)} %get-tuple-element.42) | copy-start | bytes 2949124
  147.5 159.8 %collective-permute-start.6 = (bf16[1,48,1,8,128]{1,0,4,3,2:T(2,128)(2,1)}, bf16[1,48,1,8,128]{1,0,4,3,2:T(2,128)(2,1)}, u32[]{:S(2)}, u32[]{:S(2)}) collective-permute-start(bf16[1,48,1,8,128]{1,0,4,3,2:T(2,128)(2,1)} %bitcast.90), channel_id=1, source_target_pairs={{0,32},{32,64},{64,96},{96,128},{128,160},{160,192},{192,224},{1,3... | collective-permute-start | bytes 294920 | tf_op jit(solution)/shard_map/ppermute | solution.py:17
  151.0 156.3 %collective-permute-start.7 = (bf16[1,48,1,8,128]{1,0,4,3,2:T(2,128)(2,1)}, bf16[1,48,1,8,128]{1,0,4,3,2:T(2,128)(2,1)}, u32[]{:S(2)}, u32[]{:S(2)}) collective-permute-start(bf16[1,48,1,8,128]{1,0,4,3,2:T(2,128)(2,1)} %bitcast.89), channel_id=1, source_target_pairs={{32,0},{64,32},{96,64},{128,96},{160,128},{192,160},{224,192},{33,... | collective-permute-start | bytes 294920 | tf_op jit(solution)/shard_map/ppermute | solution.py:19
  159.0 132.9 %collective-permute-start.4 = (bf16[1,48,1,8,128]{1,3,4,0,2:T(8,128)(2,1)S(1)}, bf16[1,48,1,8,128]{1,3,4,0,2:T(8,128)(2,1)S(1)}, u32[]{:S(2)}, u32[]{:S(2)}) collective-permute-start(bf16[1,48,1,8,128]{1,3,4,0,2:T(8,128)(2,1)S(1)} %slice_bitcast_fusion.3), channel_id=1, source_target_pairs={{0,32},{32,64},{64,96},{96,128},{128,160},{160,192},{192,224},{1,3... | collective-permute-start | bytes 294920 | tf_op jit(solution)/shard_map/ppermute | solution.py:17
  163.0 128.9 %collective-permute-start.5 = (bf16[1,48,1,8,128]{1,3,4,2,0:T(8,128)(2,1)S(1)}, bf16[1,48,1,8,128]{1,3,4,2,0:T(8,128)(2,1)S(1)}, u32[]{:S(2)}, u32[]{:S(2)}) collective-permute-start(bf16[1,48,1,8,128]{1,3,4,2,0:T(8,128)(2,1)S(1)} %slice_bitcast_fusion.2), channel_id=1, source_target_pairs={{32,0},{64,32},{96,64},{128,96},{160,128},{192,160},{224,192},{33,... | collective-permute-start | bytes 294920 | tf_op jit(solution)/shard_map/ppermute | solution.py:19
  304.2 3.3 copy-start.7
  304.2 5.1 copy-start.8
  309.2 110.6 %copy-start.4 = (bf16[1,48,8,8,128]{1,3,4,2,0:T(8,128)(2,1)S(1)}, bf16[1,48,8,8,128]{1,3,4,2,0:T(8,128)(2,1)}, u32[]{:S(2)}) copy-start(bf16[1,48,8,8,128]{1,3,4,2,0:T(8,128)(2,1)} %copy.85) | copy-start | bytes 2359300
  419.9 257.4 %copy-start.1 = (bf16[48,48,3,3,3]{1,0,4,3,2:T(8,128)(2,1)S(1)}, bf16[48,48,3,3,3]{1,0,4,3,2:T(8,128)(2,1)}, u32[]{:S(2)}) copy-start(bf16[48,48,3,3,3]{1,0,4,3,2:T(8,128)(2,1)} %param.8) | copy-start | bytes 373252
Sparse Core Ops, SparseCore 0:
  420.0 252.9 all-reduce.5
where the time goes:
time: 690 us; the launch traced here: 684 us
  waiting for transfers between devices  245 us (36%)
  matrix products  167 us (24%)
  blocking collectives  157 us (23%)
  local copies, waits for them, and re-layouts  66.6 us (10%)
  starting transfers between devices  20.2 us (3%)
  between operations  14.7 us (2%)
  other arithmetic  13.3 us (2%)
    psum x1, waiting for transfers between devices, local(): lax.psum((local_one, local_two, local_gain, local_bias), ('space', 'dp'))  245 us
    conv_general_dilated x2, matrix products, kernel_grad(): lax.conv_general_dilated(padded, target, (1, 1, 1), ((0, 0), (1, 1), (1,...  128 us
    psum x1, blocking collectives, local(): lax.psum((local_one, local_two, local_gain, local_bias), ('space', 'dp'))  101 us
    conv_general_dilated x3, matrix products, conv_slab(): lax.conv_general_dilated(padded, kernel, (1, 1, 1), ((0, 0), (1, 1), (1,...  39 us
    unnamed x46, local copies, waits for them, and re-layouts  36.6 us
    psum x1, blocking collectives, local(): lax.psum((jnp.sum(pre_act, axis=axes_cells, keepdims=True), jnp.sum(pre_a...  30.8 us
    psum x1, blocking collectives, local(): lax.psum((jnp.sum(grad_norm, axis=axes_cells, keepdims=True), jnp.sum(gra...  25 us
    concatenate x8, local copies, waits for them, and re-layouts, padded_2(): jnp.concatenate([lax.ppermute(tail, axis, [(i, (i + 1) % count) for i in...  20 us
  transfers between devices with their start and end apart: 9, of which 1 were waited for; matrix products, arithmetic and copies ran while one was open for 12% of the time, Pallas kernels for 0%

commit v1 on v0

v1 whole, which is shorter than its diff:
```python
import functools

import jax
import jax.numpy as jnp
from jax import lax
from jax.experimental import pallas as pl
from jax.experimental.pallas import tpu as pltpu
from jax.sharding import PartitionSpec as P

MESH = pl.DeviceIdType.MESH
F32 = jnp.float32
BF16 = jnp.bfloat16
C = 48
NZ, NX, NY = 8, 8, 128
CELLS = 64.0 * NX * NY
EPS = 1e-5
L = NX * NY
LP = L + 2 * NY
SZ_HI, SY, SX, SZ_LO = 2, 4, 4, 4
NXY = SX * SY
NZZ = SZ_HI * SZ_LO
NSP = SZ_HI * SY
ROWS = 512
HALF = ROWS // 2
PIECE = HALF // NXY


def dot(a, b):
    return lax.dot_general(a, b, (((1,), (0,)), ((), ())), preferred_element_type=F32)


def dot_nt(a, b):
    return lax.dot_general(a, b, (((1,), (1,)), ((), ())), preferred_element_type=F32)


def kernel(
    x_ref, g_ref, w1_ref, w2_ref, gain_ref, bias_ref,
    out_ref, g1_ref, g2_ref, gb_ref,
    xim, gim, him, pim, pre, gh, tmp, hx, hg, hp, w1c, w2f, w1f,
    st, acc, part, core_in, half_sum, xy_in, z_in, total,
    halo_send, halo_recv, st_send, st_recv, c_send, c_recv, xy_send, xy_recv, z_send, z_recv,
    ga_send, ga_recv, cg_send, cg_recv,
):
    sp = lax.axis_index("space")
    dp = lax.axis_index("dp")
    z_hi, y = sp // SY, sp % SY
    xx_, z_lo, core = dp // (SZ_LO * 2), (dp // 2) % SZ_LO, dp % 2
    me_xy = xx_ * SY + y
    me_z = z_hi * SZ_LO + z_lo
    sibling = (sp, dp + 1 - 2 * core)

    def sp_dev(j):
        return (j, dp)

    def xy_dev(j):
        return (z_hi * SY + j % SY, (j // SY) * (SZ_LO * 2) + z_lo * 2 + core)

    def z_dev(j):
        return ((j // SZ_LO) * SY + y, xx_ * (SZ_LO * 2) + (j % SZ_LO) * 2 + core)

    def others(count, me, body):
        def step(k, carry):
            body(lax.rem(me + k, count))
            return carry
        lax.fori_loop(1, count, step, 0)

    barrier = pltpu.get_barrier_semaphore()

    def greet(dev):
        pl.semaphore_signal(barrier, inc=1, device_id=dev, device_id_type=MESH)

    greet(sibling)
    others(NSP, sp, lambda j: greet(sp_dev(j)))
    others(NXY, me_xy, lambda j: greet(xy_dev(j)))
    others(NZZ, me_z, lambda j: greet(z_dev(j)))

    lane = lax.broadcasted_iota(jnp.int32, (C, NY), 1)
    eye = lax.broadcasted_iota(jnp.int32, (C, NY), 0) == lane
    first, last = lane == 0, lane == NY - 1

    def column(row):
        return jnp.sum(jnp.where(eye, jnp.broadcast_to(row, (C, NY)), 0.0), axis=1, keepdims=True)

    def as_row(col):
        return jnp.sum(jnp.where(eye, jnp.broadcast_to(col, (C, NY)), 0.0), axis=0, keepdims=True)

    def put(im, zi, lo, v):
        at = pl.ds(lo, NY)
        im[zi, 0:C, at] = jnp.where(first, 0.0, pltpu.roll(v, 1, 1)).astype(BF16)
        im[zi, C : 2 * C, at] = v.astype(BF16)
        im[zi, 2 * C : 3 * C, at] = jnp.where(last, 0.0, pltpu.roll(v, NY - 1, 1)).astype(BF16)

    def unpack(raw, im, zi, live):
        plane = raw.astype(F32)
        if live is not None:
            plane = jnp.where(live, plane, 0.0)
        tmp[...] = plane.reshape(C * NX, NY)
        for xb in range(NX):
            put(im, zi, NY * (xb + 1), tmp[pl.ds(xb, C, stride=NX), :])

    edge = jnp.zeros((3 * C, NY), BF16)

    def zero_edges(zi, carry):
        for im in (xim, gim, pim):
            im[zi, :, 0:NY] = edge
            im[zi, :, LP - NY : LP] = edge
        return carry

    lax.fori_loop(0, NZ + 2, zero_edges, 0)
    pim[0, C : 2 * C, :] = jnp.zeros((C, LP), BF16)
    pim[NZ + 1, C : 2 * C, :] = jnp.zeros((C, LP), BF16)

    def unpack_own(src, im):
        def step(zi, carry):
            unpack(src[:, pl.ds(zi, 1)].reshape(C, NX, NY), im, zi + 1, None)
            return carry
        lax.fori_loop(0, NZ, step, 0)

    unpack_own(x_ref, xim)

    for dz in range(3):
        rows = slice(dz * C, (dz + 1) * C)
        blocks = [w1_ref[dz * 9 + t].astype(F32).T for t in range(9)]
        w1c[rows, :] = jnp.concatenate(blocks, axis=0).T.astype(BF16)
        for w_ref, dst in ((w2_ref, w2f), (w1_ref, w1f)):
            blocks = [w_ref[26 - (dz * 9 + t)].astype(F32) for t in range(9)]
            dst[rows, :] = jnp.concatenate(blocks, axis=0).T.astype(BF16)

    pl.semaphore_wait(barrier, 1 + (NSP - 1) + (NXY - 1) + (NZZ - 1))

    has_up, has_down = sp < NSP - 1, sp > 0

    def halo_copy(src, dst, k, slot, dev):
        return pltpu.make_async_remote_copy(
            src_ref=src, dst_ref=dst.at[slot], send_sem=halo_send.at[k, slot],
            recv_sem=halo_recv.at[k, slot], device_id=dev, device_id_type=MESH,
        )

    def halo_start(low, high, dst, k):
        @pl.when(has_up)
        def _():
            halo_copy(high, dst, k, 0, (sp + 1, dp)).start()

        @pl.when(has_down)
        def _():
            halo_copy(low, dst, k, 1, (sp - 1, dp)).start()

    def halo_wait(low, high, dst, k):
        @pl.when(has_up)
        def _():
            halo_copy(high, dst, k, 0, (sp + 1, dp)).wait_send()
            halo_copy(high, dst, k, 1, (sp + 1, dp)).wait_recv()

        @pl.when(has_down)
        def _():
            halo_copy(low, dst, k, 1, (sp - 1, dp)).wait_send()
            halo_copy(low, dst, k, 0, (sp - 1, dp)).wait_recv()

    x_halo = (x_ref.at[:, 0], x_ref.at[:, NZ - 1], hx, 0)
    g_halo = (g_ref.at[:, 0], g_ref.at[:, NZ - 1], hg, 1)
    halo_start(*x_halo)
    halo_start(*g_halo)

    def window(im, zi):
        return jnp.concatenate([im[zi, :, NY * d : NY * d + L] for d in range(3)], axis=0)

    def conv_inner(im, w, dst):
        dst[0] = jnp.zeros((C, L), F32)
        dst[1] = jnp.zeros((C, L), F32)

        def step(zi, carry):
            p = dot(w[...], window(im, zi))
            dst[zi + 1] = p[0:C]
            dst[zi] += p[C : 2 * C]
            dst[zi - 1] += p[2 * C : 3 * C]
            return carry

        lax.fori_loop(1, NZ + 1, step, 0)

    def conv_faces(im, w, dst):
        dst[1] += dot(w[0:C], window(im, 0))
        dst[NZ] += dot(w[2 * C : 3 * C], window(im, NZ + 1))

    def face_planes(dst, im):
        unpack(dst[0], im, 0, has_down)
        unpack(dst[1], im, NZ + 1, has_up)

    def st_copy(k, j):
        return pltpu.make_async_remote_copy(
            src_ref=st.at[k, sp], dst_ref=st.at[k, sp], send_sem=st_send.at[k, j],
            recv_sem=st_recv.at[k, sp], device_id=sp_dev(j), device_id_type=MESH,
        )

    def st_wait(k, j):
        return pltpu.make_async_remote_copy(
            src_ref=st.at[k, j], dst_ref=st.at[k, j], send_sem=st_send.at[k, j],
            recv_sem=st_recv.at[k, j], device_id=sp_dev(j), device_id_type=MESH,
        )

    def st_start(k, one, two):
        row_one = as_row(jnp.sum(one, axis=1, keepdims=True))
        row_two = as_row(jnp.sum(two, axis=1, keepdims=True))
        lead = lax.broadcasted_iota(jnp.int32, (8, NY), 0)
        mine = jnp.where(lead == 0, row_one, 0.0) + jnp.where(lead == 1, row_two, 0.0)
        st[k, sp] = mine
        others(NSP, sp, lambda j: st_copy(k, j).start())
        return mine

    def st_finish(k):
        others(NSP, sp, lambda j: st_wait(k, j).wait_recv())
        others(NSP, sp, lambda j: st_copy(k, j).wait_send())
        s = st[k, 0]
        for j in range(1, NSP):
            s = s + st[k, j]
        return column(s[0:1] / CELLS), column(s[1:2] / CELLS)

    conv_inner(xim, w1c, pre)
    halo_wait(*x_halo)
    face_planes(hx, xim)
    conv_faces(xim, w1c, pre)

    zero = jnp.zeros((C, NY), F32)

    def moments(zi, carry):
        one, two = carry
        for xb in range(NX):
            v = pre[zi, :, NY * xb : NY * (xb + 1)]
            one, two = one + v, two + v * v
        return one, two

    st_start(0, *lax.fori_loop(1, NZ + 1, moments, (zero, zero)))

    unpack_own(g_ref, gim)
    conv_inner(gim, w2f, gh)
    halo_wait(*g_halo)
    face_planes(hg, gim)
    conv_faces(gim, w2f, gh)

    pad = jnp.zeros((1, NY - C), F32)
    gain = column(jnp.concatenate([gain_ref[...], pad], axis=1))
    bias = column(jnp.concatenate([bias_ref[...], pad], axis=1))
    mean, square = st_finish(0)
    inv_std = lax.rsqrt(square - mean * mean + EPS)

    def activate(zi, carry):
        one, two = carry
        for xb in range(NX):
            at = slice(NY * xb, NY * (xb + 1))
            hat = (pre[zi, :, at] - mean) * inv_std
            normed = hat * gain + bias
            sig = jax.nn.sigmoid(normed)
            put(him, zi - 1, NY * xb, (normed * sig).astype(BF16).astype(F32))
            gn = gh[zi, :, at] * sig * (1.0 + normed * (1.0 - sig))
            gh[zi, :, at] = gn
            pre[zi, :, at] = hat
            one, two = one + gn, two + gn * hat
        return one, two

    slopes = st_start(1, *lax.fori_loop(1, NZ + 1, activate, (zero, zero)))

    def c_copy(k):
        return pltpu.make_async_remote_copy(
            src_ref=part.at[k, pl.ds((1 - core) * HALF, HALF)], dst_ref=core_in.at[k],
            send_sem=c_send.at[k], recv_sem=c_recv.at[k], device_id=sibling, device_id_type=MESH,
        )

    def pack(k, tail):
        main = acc[:, 0:NY]
        part[k, 0 : 9 * C] = main
        rest = acc[:, NY : NY + 16]
        pieces = [rest[64 * r : 64 * (r + 1)] for r in range(6)]
        pieces.append(jnp.concatenate([rest[384:432], jnp.zeros((16, 16), F32)], axis=0))
        pieces.append(jnp.zeros((64, 16), F32))
        part[k, 9 * C : 9 * C + 64] = jnp.concatenate(pieces, axis=1)
        part[k, 496:504] = tail
        part[k, 504:512] = jnp.zeros((8, NY), F32)

    def core_start(k):
        c_copy(k).start()

    def xy_copy(k, j):
        return pltpu.make_async_remote_copy(
            src_ref=half_sum.at[k, pl.ds(j * PIECE, PIECE)], dst_ref=xy_in.at[k, me_xy],
            send_sem=xy_send.at[k, j], recv_sem=xy_recv.at[k, me_xy], device_id=xy_dev(j), device_id_type=MESH,
        )

    def xy_wait(k, j):
        return pltpu.make_async_remote_copy(
            src_ref=xy_in.at[k, j], dst_ref=xy_in.at[k, j],
            send_sem=xy_send.at[k, j], recv_sem=xy_recv.at[k, j], device_id=xy_dev(j), device_id_type=MESH,
        )

    def core_finish(k):
        c_copy(k).wait()
        half_sum[k] = part[k, pl.ds(core * HALF, HALF)] + core_in[k]
        others(NXY, me_xy, lambda j: xy_copy(k, j).start())

    def z_copy(k, j):
        return pltpu.make_async_remote_copy(
            src_ref=z_in.at[k, me_z], dst_ref=z_in.at[k, me_z],
            send_sem=z_send.at[k, j], recv_sem=z_recv.at[k, me_z], device_id=z_dev(j), device_id_type=MESH,
        )

    def z_wait(k, j):
        return pltpu.make_async_remote_copy(
            src_ref=z_in.at[k, j], dst_ref=z_in.at[k, j],
            send_sem=z_send.at[k, j], recv_sem=z_recv.at[k, j], device_id=z_dev(j), device_id_type=MESH,
        )

    def xy_finish(k):
        others(NXY, me_xy, lambda j: xy_wait(k, j).wait_recv())
        xy_in[k, me_xy] = half_sum[k, pl.ds(me_xy * PIECE, PIECE)]
        s = xy_in[k, 0]
        for j in range(1, NXY):
            s = s + xy_in[k, j]
        z_in[k, me_z] = s
        others(NZZ, me_z, lambda j: z_copy(k, j).start())

    def ga_at(j):
        return pl.ds(core * HALF + j * PIECE, PIECE)

    def ga_copy(k, j):
        return pltpu.make_async_remote_copy(
            src_ref=total.at[k, ga_at(me_xy)], dst_ref=total.at[k, ga_at(me_xy)],
            send_sem=ga_send.at[k, j], recv_sem=ga_recv.at[k, me_xy], device_id=xy_dev(j), device_id_type=MESH,
        )

    def ga_wait(k, j):
        return pltpu.make_async_remote_copy(
            src_ref=total.at[k, ga_at(j)], dst_ref=total.at[k, ga_at(j)],
            send_sem=ga_send.at[k, j], recv_sem=ga_recv.at[k, j], device_id=xy_dev(j), device_id_type=MESH,
        )

    def z_finish(k):
        others(NZZ, me_z, lambda j: z_wait(k, j).wait_recv())
        s = z_in[k, 0]
        for j in range(1, NZZ):
            s = s + z_in[k, j]
        total[k, ga_at(me_xy)] = s
        others(NXY, me_xy, lambda j: ga_copy(k, j).start())

    def cg_copy(k, which):
        at = pl.ds(which * HALF, HALF)
        return pltpu.make_async_remote_copy(
            src_ref=total.at[k, at], dst_ref=total.at[k, at],
            send_sem=cg_send.at[k], recv_sem=cg_recv.at[k], device_id=sibling, device_id_type=MESH,
        )

    def gather_finish(k):
        others(NXY, me_xy, lambda j: ga_wait(k, j).wait_recv())
        cg_copy(k, core).start()

    def drain(k):
        others(NXY, me_xy, lambda j: xy_copy(k, j).wait_send())
        others(NXY, me_xy, lambda j: ga_copy(k, j).wait_send())
        others(NZZ, me_z, lambda j: z_copy(k, j).wait_send())

    def all_finish(k, dst):
        cg_copy(k, core).wait_send()
        cg_copy(k, 1 - core).wait_recv()
        for b in range(9):
            m = total[k, b * C : (b + 1) * C]
            dst[3 * b] = m[:, 0:C]
            dst[3 * b + 1] = m[:, C : 2 * C]
            r, o = (b * C) // 64, (b * C) % 64
            rows = []
            left = C
            while left:
                n = min(64 - o, left)
                rows.append(total[k, 9 * C + o : 9 * C + o + n, 16 * r : 16 * (r + 1)])
                left -= n
                r, o = r + 1, 0
            tail = rows[0] if len(rows) == 1 else jnp.concatenate(rows, axis=0)
            dst[3 * b + 2] = jnp.concatenate([m[:, 2 * C : NY], tail], axis=1)

    acc[...] = jnp.zeros((9 * C, 3 * C), F32)

    def grad_two(zi, carry):
        lhs = jnp.concatenate(
            [
                gim[zi + 2 - dz, C : 2 * C, NY * (2 - dx) : NY * (2 - dx) + L]
                for dz in range(3)
                for dx in range(3)
            ],
            axis=0,
        )
        acc[...] += dot_nt(lhs, him[zi])
        return carry

    lax.fori_loop(0, NZ, grad_two, 0)
    pack(0, slopes)
    core_start(0)

    slope, slope_dot = st_finish(1)
    scale = gain * inv_std

    def before(zi, carry):
        for xb in range(NX):
            at = slice(NY * xb, NY * (xb + 1))
            gp = scale * (gh[zi, :, at] - slope - pre[zi, :, at] * slope_dot)
            put(pim, zi, NY * (xb + 1), gp.astype(BF16).astype(F32))
        return carry

    lax.fori_loop(1, NZ + 1, before, 0)
    p_halo = (pim.at[1, C : 2 * C, NY : NY + L], pim.at[NZ, C : 2 * C, NY : NY + L], hp, 2)
    halo_start(*p_halo)
    core_finish(0)

    acc[...] = jnp.zeros((9 * C, 3 * C), F32)

    def grad_one_rows(zi, dzs):
        return jnp.concatenate(
            [
                pim[zi + 1 - dz, C : 2 * C, NY * (2 - dx) : NY * (2 - dx) + L]
                for dz in dzs
                for dx in range(3)
            ],
            axis=0,
        )

    def grad_one(zi, carry):
        acc[...] += dot_nt(grad_one_rows(zi, range(3)), xim[zi, :, NY : NY + L])
        return carry

    lax.fori_loop(1, NZ + 1, grad_one, 0)
    acc[0 : 3 * C] += dot_nt(grad_one_rows(0, (0,)), xim[0, :, NY : NY + L])
    acc[6 * C : 9 * C] += dot_nt(grad_one_rows(NZ + 1, (2,)), xim[NZ + 1, :, NY : NY + L])
    pack(1, jnp.zeros((8, NY), F32))
    core_start(1)
    xy_finish(0)

    core_finish(1)
    conv_inner(pim, w1f, gh)
    z_finish(0)
    xy_finish(1)
    halo_wait(*p_halo)

    def face_plane(slot, zi, live):
        for xb in range(NX):
            v = hp[slot, :, NY * xb : NY * (xb + 1)].astype(F32)
            put(pim, zi, NY * (xb + 1), jnp.where(live, v, 0.0))

    face_plane(0, 0, has_down)
    face_plane(1, NZ + 1, has_up)
    conv_faces(pim, w1f, gh)
    z_finish(1)

    def finish(zi, carry):
        for xb in range(NX):
            v = gh[zi, :, NY * xb : NY * (xb + 1)]
            up = gim[zi, C : 2 * C, NY * (xb + 1) : NY * (xb + 2)]
            tmp[pl.ds(xb, C, stride=NX), :] = v + up.astype(F32)
        out_ref[:, pl.ds(zi - 1, 1)] = tmp[...].reshape(C, 1, NX, NY).astype(BF16)
        return carry

    lax.fori_loop(1, NZ + 1, finish, 0)
    gather_finish(0)
    gather_finish(1)
    all_finish(0, g2_ref)
    gb_ref[...] = total[0, 496:504]
    all_finish(1, g1_ref)
    drain(0)
    drain(1)


def local(features, upstream, weight_one, weight_two, norm_gain, norm_bias):
    w1 = jnp.transpose(weight_one, (2, 3, 4, 0, 1)).reshape(27, C, C)
    w2 = jnp.transpose(weight_two, (2, 3, 4, 0, 1)).reshape(27, C, C)
    vmem = pl.BlockSpec(memory_space=pltpu.VMEM)
    dma = pltpu.SemaphoreType.DMA
    out, g1, g2, gb = pl.pallas_call(
        kernel,
        out_shape=(
            jax.ShapeDtypeStruct((C, NZ, NX, NY), BF16),
            jax.ShapeDtypeStruct((27, C, C), F32),
            jax.ShapeDtypeStruct((27, C, C), F32),
            jax.ShapeDtypeStruct((8, NY), F32),
        ),
        in_specs=[vmem] * 6,
        out_specs=(vmem,) * 4,
        scratch_shapes=[
            pltpu.VMEM((NZ + 2, 3 * C, LP), BF16),
            pltpu.VMEM((NZ + 2, 3 * C, LP), BF16),
            pltpu.VMEM((NZ, 3 * C, L), BF16),
            pltpu.VMEM((NZ + 2, 3 * C, LP), BF16),
            pltpu.VMEM((NZ + 2, C, L), F32),
            pltpu.VMEM((NZ + 2, C, L), F32),
            pltpu.VMEM((C * NX, NY), F32),
            pltpu.VMEM((2, C, NX, NY), BF16),
            pltpu.VMEM((2, C, NX, NY), BF16),
            pltpu.VMEM((2, C, L), BF16),
            pltpu.VMEM((3 * C, 9 * C), BF16),
            pltpu.VMEM((3 * C, 9 * C), BF16),
            pltpu.VMEM((3 * C, 9 * C), BF16),
            pltpu.VMEM((2, NSP, 8, NY), F32),
            pltpu.VMEM((9 * C, 3 * C), F32),
            pltpu.VMEM((2, ROWS, NY), F32),
            pltpu.VMEM((2, HALF, NY), F32),
            pltpu.VMEM((2, HALF, NY), F32),
            pltpu.VMEM((2, NXY, PIECE, NY), F32),
            pltpu.VMEM((2, NZZ, PIECE, NY), F32),
            pltpu.VMEM((2, ROWS, NY), F32),
            dma((3, 2)), dma((3, 2)),
            dma((2, NSP)), dma((2, NSP)),
            dma((2,)), dma((2,)),
            dma((2, NXY)), dma((2, NXY)),
            dma((2, NZZ)), dma((2, NZZ)),
            dma((2, NXY)), dma((2, NXY)),
            dma((2,)), dma((2,)),
        ],
        compiler_params=pltpu.CompilerParams(
            collective_id=0, has_side_effects=True, vmem_limit_bytes=56 * 1024 * 1024
        ),
    )(
        features.reshape(C, NZ, NX, NY),
        upstream.reshape(C, NZ, NX, NY),
        w1,
        w2,
        norm_gain.reshape(1, C),
        norm_bias.reshape(1, C),
    )

    def grad(m):
        return jnp.transpose(m.reshape(3, 3, 3, C, C), (3, 4, 0, 1, 2))

    return out.reshape(1, C, NZ, NX, NY), grad(g1), grad(g2), gb[1, :C], gb[0, :C]


def solution(mesh):
    cells = P("dp", None, "space", None, None)
    return jax.shard_map(
        local,
        mesh=mesh,
        in_specs=(cells, cells, P(), P(), P(), P()),
        out_specs=(cells, P(), P(), P(), P()),
        check_vma=False,
    )
```

time: 690 us -> 73.1 us (0.11)
  waiting for transfers between devices: 245 us -> 0 us
  matrix products: 167 us -> 0 us
  blocking collectives: 157 us -> 0 us
  Pallas kernels: 0 us -> 66.6 us
  local copies, waits for them, and re-layouts: 66.6 us -> 5.58 us
  starting transfers between devices: 20.2 us -> 0 us
  between operations: 14.7 us -> 0.64 us
  other arithmetic: 13.3 us -> 0 us
    psum x1 -> x0, waiting for transfers between devices: 245 us -> none  [local(): lax.psum((local_one, local_two, local_gain, local_bias), ('space', 'dp'))]
    conv_general_dilated x5 -> x0, matrix products: 167 us -> none  [the longest x2 128 us: kernel_grad(): lax.conv_general_dilated(padded, target, (1, 1, 1), ((0, 0), (1, 1), (1,...]
    psum x3 -> x0, blocking collectives: 157 us -> none  [the longest x1 101 us: local(): lax.psum((local_one, local_two, local_gain, local_bias), ('space', 'dp'))]
    pallas_call x0 -> x1, Pallas kernels: none -> 66.6 us  [local(): pl.pallas_call(kernel, out_shape=(jax.ShapeDtypeStruct((C, NZ, NX, NY), B...]
    unnamed x46 -> x7, local copies, waits for them, and re-layouts: 36.6 us -> 4.3 us
    ppermute x8 -> x0, starting transfers between devices: 20.1 us -> none  [the longest x4 15 us: padded_2(): lax.ppermute(tail, axis, [(i, (i + 1) % count) for i in range(ends)])]
    concatenate x8 -> x0, local copies, waits for them, and re-layouts: 20 us -> none  [padded_2(): jnp.concatenate([lax.ppermute(tail, axis, [(i, (i + 1) % count) for i in...]
    convert_element_type x2 -> x0, other arithmetic: 8.99 us -> none  [the longest x1 4.86 us: local(): hidden = (normed * sigmoid_val).astype(jnp.bfloat16)]
  transfers between devices with their start and end apart: 9 -> 0, of which waited for: 1 -> 0; matrix products, arithmetic and copies ran while one was open for 12% -> 0% of each run, Pallas kernels for 0% -> 0%
where the time goes in v1:
time: 73.1 us; the launch traced here: 72.8 us
  Pallas kernels  66.6 us (91%)
  local copies, waits for them, and re-layouts  5.58 us (8%)
    pallas_call x1, Pallas kernels, local(): pl.pallas_call(kernel, out_shape=(jax.ShapeDtypeStruct((C, NZ, NX, NY), B...  66.6 us
    unnamed x7, local copies, waits for them, and re-layouts  4.3 us

profile of v1, /device:TPU:1, one launch (start us, length us, event | category | flops | bytes accessed | tf_op | source)
XLA Modules:
  0.0 72.8 jit_solution(18140694841985402647)
XLA Ops:
  0.6 66.6 %shard_map.101 = (bf16[48,8,8,128]{3,2,1,0:T(8,128)(2,1)}, f32[27,48,48]{2,1,0:T(8,128)}, f32[27,48,48]{2,1,0:T(8,128)}, f32[8,128]{1,0:T(8,128)}) custom-call(bf16[48,8,8,128]{3,2,1,0:T(8,128)(2,1)} %bitcast.22, bf16[48,8,8,128]{3,2,1,0:T(8,128)(2,1)} %bitcast.23, bf16[27,48,48]{2,1,0:T(8,128)(2,1)} %bitcast.26, bf16[27,48,48]{2,1,0:T(8,128)(2,1)} %bitcast.27, ...), custom_call_target="tpu_custom_call" | custom-call | tf_op jit(solution)/shard_map/pallas_call | solution.py:471
  67.2 1.3 %slice_bitcast_fusion = (f32[48]{0:T(128)}, f32[48]{0:T(128)}) fusion(f32[8,128]{1,0:T(8,128)} %get-tuple-element.12), kind=kLoop, calls=%fused_computation | loop fusion | bytes 768 | tf_op jit(solution)/shard_map/squeeze | solution.py:526
  68.5 0.0 copy-start.1
  68.5 2.1 %copy.14 = bf16[1,48,8,8,128]{4,3,2,1,0:T(8,128)(2,1)} copy(bf16[1,48,8,8,128]{4,3,2,1,0:T(8,128)(2,1)} %bitcast.21) | data formatting | bytes 1572864
  70.7 0.0 copy-done.1
  70.7 0.0 copy-start
  70.7 0.8 %copy.15 = f32[48,48,3,3,3]{1,0,4,3,2:T(8,128)} copy(f32[48,48,3,3,3]{1,0,4,3,2:T(8,128)S(1)} %bitcast.25) | data formatting | bytes 497664
  71.5 0.5 copy-done
  72.0 0.8 %copy.16 = f32[48,48,3,3,3]{1,0,4,3,2:T(8,128)} copy(f32[48,48,3,3,3]{1,0,4,3,2:T(8,128)S(1)} %bitcast.24) | data formatting | bytes 497664
Async XLA Ops:
  68.5 2.1 %copy-start.1 = (f32[27,48,48]{2,1,0:T(8,128)S(1)}, f32[27,48,48]{2,1,0:T(8,128)}, u32[]{:S(2)}) copy-start(f32[27,48,48]{2,1,0:T(8,128)} %get-tuple-element.10) | copy-start | bytes 746500
  70.7 1.3 %copy-start = (f32[27,48,48]{2,1,0:T(8,128)S(1)}, f32[27,48,48]{2,1,0:T(8,128)}, u32[]{:S(2)}) copy-start(f32[27,48,48]{2,1,0:T(8,128)} %get-tuple-element.11) | copy-start | bytes 746500

commit v2 on v1

--- a/solution.py
+++ b/solution.py
@@ -34,10 +34,11 @@
 
 
 def kernel(
-    x_ref, g_ref, w1_ref, w2_ref, gain_ref, bias_ref,
-    out_ref, g1_ref, g2_ref, gb_ref,
+    x_hbm, g_hbm, w1_hbm, w2_hbm, gain_ref, bias_ref,
+    out_ref, total,
+    x_ref, g_ref, w1_ref, w2_ref, load,
     xim, gim, him, pim, pre, gh, tmp, hx, hg, hp, w1c, w2f, w1f,
-    st, acc, part, core_in, half_sum, xy_in, z_in, total,
+    st, acc, part, core_in, half_sum, xy_in, z_in,
     halo_send, halo_recv, st_send, st_recv, c_send, c_recv, xy_send, xy_recv, z_send, z_recv,
     ga_send, ga_recv, cg_send, cg_recv,
 ):
@@ -64,6 +65,15 @@
             return carry
         lax.fori_loop(1, count, step, 0)
 
+    loads = [
+        pltpu.make_async_copy(src, dst, load.at[i])
+        for i, (src, dst) in enumerate(
+            ((x_hbm, x_ref), (w1_hbm, w1_ref), (w2_hbm, w2_ref), (g_hbm, g_ref))
+        )
+    ]
+    for each in loads:
+        each.start()
+
     barrier = pltpu.get_barrier_semaphore()
 
     def greet(dev):
@@ -84,11 +94,22 @@
     def as_row(col):
         return jnp.sum(jnp.where(eye, jnp.broadcast_to(col, (C, NY)), 0.0), axis=0, keepdims=True)
 
+    def put_sides(im, zi, at, v):
+        im[zi, 0:C, at] = jnp.where(first, 0.0, pltpu.roll(v, 1, 1)).astype(BF16)
+        im[zi, 2 * C : 3 * C, at] = jnp.where(last, 0.0, pltpu.roll(v, NY - 1, 1)).astype(BF16)
+
     def put(im, zi, lo, v):
         at = pl.ds(lo, NY)
-        im[zi, 0:C, at] = jnp.where(first, 0.0, pltpu.roll(v, 1, 1)).astype(BF16)
         im[zi, C : 2 * C, at] = v.astype(BF16)
-        im[zi, 2 * C : 3 * C, at] = jnp.where(last, 0.0, pltpu.roll(v, NY - 1, 1)).astype(BF16)
+        put_sides(im, zi, at, v)
+
+    def sides(im, begin, lo):
+        def step(zi, carry):
+            for xb in range(NX):
+                at = pl.ds(lo + NY * xb, NY)
+                put_sides(im, zi, at, im[zi, C : 2 * C, at].astype(F32))
+            return carry
+        lax.fori_loop(begin, begin + NZ, step, 0)
 
     def unpack(raw, im, zi, live):
         plane = raw.astype(F32)
@@ -116,8 +137,11 @@
             return carry
         lax.fori_loop(0, NZ, step, 0)
 
+    loads[0].wait()
     unpack_own(x_ref, xim)
 
+    loads[1].wait()
+    loads[2].wait()
     for dz in range(3):
         rows = slice(dz * C, (dz + 1) * C)
         blocks = [w1_ref[dz * 9 + t].astype(F32).T for t in range(9)]
@@ -126,8 +150,6 @@
             blocks = [w_ref[26 - (dz * 9 + t)].astype(F32) for t in range(9)]
             dst[rows, :] = jnp.concatenate(blocks, axis=0).T.astype(BF16)
 
-    pl.semaphore_wait(barrier, 1 + (NSP - 1) + (NXY - 1) + (NZZ - 1))
-
     has_up, has_down = sp < NSP - 1, sp > 0
 
     def halo_copy(src, dst, k, slot, dev):
@@ -158,8 +180,6 @@
 
     x_halo = (x_ref.at[:, 0], x_ref.at[:, NZ - 1], hx, 0)
     g_halo = (g_ref.at[:, 0], g_ref.at[:, NZ - 1], hg, 1)
-    halo_start(*x_halo)
-    halo_start(*g_halo)
 
     def window(im, zi):
         return jnp.concatenate([im[zi, :, NY * d : NY * d + L] for d in range(3)], axis=0)
@@ -215,6 +235,13 @@
         return column(s[0:1] / CELLS), column(s[1:2] / CELLS)
 
     conv_inner(xim, w1c, pre)
+    loads[3].wait()
+    unpack_own(g_ref, gim)
+    pl.semaphore_wait(barrier, 1 + (NSP - 1) + (NXY - 1) + (NZZ - 1))
+
+    halo_start(*x_halo)
+    halo_start(*g_halo)
+    conv_inner(gim, w2f, gh)
     halo_wait(*x_halo)
     face_planes(hx, xim)
     conv_faces(xim, w1c, pre)
@@ -230,8 +257,6 @@
 
     st_start(0, *lax.fori_loop(1, NZ + 1, moments, (zero, zero)))
 
-    unpack_own(g_ref, gim)
-    conv_inner(gim, w2f, gh)
     halo_wait(*g_halo)
     face_planes(hg, gim)
     conv_faces(gim, w2f, gh)
@@ -249,7 +274,7 @@
             hat = (pre[zi, :, at] - mean) * inv_std
             normed = hat * gain + bias
             sig = jax.nn.sigmoid(normed)
-            put(him, zi - 1, NY * xb, (normed * sig).astype(BF16).astype(F32))
+            him[zi - 1, C : 2 * C, at] = (normed * sig).astype(BF16)
             gn = gh[zi, :, at] * sig * (1.0 + normed * (1.0 - sig))
             gh[zi, :, at] = gn
             pre[zi, :, at] = hat
@@ -355,9 +380,105 @@
         others(NXY, me_xy, lambda j: ga_copy(k, j).wait_send())
         others(NZZ, me_z, lambda j: z_copy(k, j).wait_send())
 
-    def all_finish(k, dst):
+    def all_finish(k):
         cg_copy(k, core).wait_send()
         cg_copy(k, 1 - core).wait_recv()
+
+    sides(him, 0, 0)
+    acc[...] = jnp.zeros((9 * C, 3 * C), F32)
+
+    def shifted(im, zi, dzs):
+        return jnp.concatenate(
+            [
+                im[zi + 1 - dz, C : 2 * C, NY * (2 - dx) : NY * (2 - dx) + L]
+                for dz in dzs
+                for dx in range(3)
+            ],
+            axis=0,
+        )
+
+    def pair(im, zi):
+        return jnp.concatenate([shifted(im, zi, range(3)), shifted(im, zi + 1, range(3))], axis=1)
+
+    def grad_two(i, carry):
+        zi = 2 * i
+        acc[...] += dot_nt(pair(gim, zi + 1), jnp.concatenate([him[zi], him[zi + 1]], axis=1))
+        return carry
+
+    lax.fori_loop(0, NZ // 2, grad_two, 0)
+    pack(0, slopes)
+    core_start(0)
+
+    slope, slope_dot = st_finish(1)
+    core_finish(0)
+    scale = gain * inv_std
+
+    def before(zi, carry):
+        for xb in range(NX):
+            at = slice(NY * xb, NY * (xb + 1))
+            gp = scale * (gh[zi, :, at] - slope - pre[zi, :, at] * slope_dot)
+            pim[zi, C : 2 * C, NY * (xb + 1) : NY * (xb + 2)] = gp.astype(BF16)
+        return carry
+
+    lax.fori_loop(1, NZ + 1, before, 0)
+    p_halo = (pim.at[1, C : 2 * C, NY : NY + L], pim.at[NZ, C : 2 * C, NY : NY + L], hp, 2)
+    halo_start(*p_halo)
+
+    acc[...] = jnp.zeros((9 * C, 3 * C), F32)
+
+    def grad_one(i, carry):
+        zi = 2 * i + 1
+        at = slice(NY, NY + L)
+        acc[...] += dot_nt(pair(pim, zi), jnp.concatenate([xim[zi, :, at], xim[zi + 1, :, at]], axis=1))
+        return carry
+
+    lax.fori_loop(0, NZ // 2, grad_one, 0)
+    acc[0 : 3 * C] += dot_nt(shifted(pim, 0, (0,)), xim[0, :, NY : NY + L])
+    acc[6 * C : 9 * C] += dot_nt(shifted(pim, NZ + 1, (2,)), xim[NZ + 1, :, NY : NY + L])
+    pack(1, jnp.zeros((8, NY), F32))
+    core_start(1)
+
+    sides(pim, 1, NY)
+    core_finish(1)
+    conv_inner(pim, w1f, gh)
+    xy_finish(0)
+    xy_finish(1)
+    halo_wait(*p_halo)
+
+    def face_plane(slot, zi, live):
+        for xb in range(NX):
+            v = hp[slot, :, NY * xb : NY * (xb + 1)].astype(F32)
+            put(pim, zi, NY * (xb + 1), jnp.where(live, v, 0.0))
+
+    face_plane(0, 0, has_down)
+    face_plane(1, NZ + 1, has_up)
+    conv_faces(pim, w1f, gh)
+
+    def finish(zi, carry):
+        for xb in range(NX):
+            v = gh[zi, :, NY * xb : NY * (xb + 1)]
+            up = gim[zi, C : 2 * C, NY * (xb + 1) : NY * (xb + 2)]
+            tmp[pl.ds(xb, C, stride=NX), :] = v + up.astype(F32)
+        out_ref[:, pl.ds(zi - 1, 1)] = tmp[...].reshape(C, 1, NX, NY).astype(BF16)
+        return carry
+
+    lax.fori_loop(1, NZ + 1, finish, 0)
+    z_finish(0)
+    z_finish(1)
+    gather_finish(0)
+    gather_finish(1)
+    all_finish(0)
+    all_finish(1)
+    drain(0)
+    drain(1)
+
+
+def results(
+    raw, total, out_ref, g1_ref, g2_ref, gain_ref, bias_ref, sem
+):
+    copy = pltpu.make_async_copy(raw, out_ref, sem)
+    copy.start()
+    for k, dst in ((0, g2_ref), (1, g1_ref)):
         for b in range(9):
             m = total[k, b * C : (b + 1) * C]
             dst[3 * b] = m[:, 0:C]
@@ -372,95 +493,9 @@
                 r, o = r + 1, 0
             tail = rows[0] if len(rows) == 1 else jnp.concatenate(rows, axis=0)
             dst[3 * b + 2] = jnp.concatenate([m[:, 2 * C : NY], tail], axis=1)
-
-    acc[...] = jnp.zeros((9 * C, 3 * C), F32)
-
-    def grad_two(zi, carry):
-        lhs = jnp.concatenate(
-            [
-                gim[zi + 2 - dz, C : 2 * C, NY * (2 - dx) : NY * (2 - dx) + L]
-                for dz in range(3)
-                for dx in range(3)
-            ],
-            axis=0,
-        )
-        acc[...] += dot_nt(lhs, him[zi])
-        return carry
-
-    lax.fori_loop(0, NZ, grad_two, 0)
-    pack(0, slopes)
-    core_start(0)
-
-    slope, slope_dot = st_finish(1)
-    scale = gain * inv_std
-
-    def before(zi, carry):
-        for xb in range(NX):
-            at = slice(NY * xb, NY * (xb + 1))
-            gp = scale * (gh[zi, :, at] - slope - pre[zi, :, at] * slope_dot)
-            put(pim, zi, NY * (xb + 1), gp.astype(BF16).astype(F32))
-        return carry
-
-    lax.fori_loop(1, NZ + 1, before, 0)
-    p_halo = (pim.at[1, C : 2 * C, NY : NY + L], pim.at[NZ, C : 2 * C, NY : NY + L], hp, 2)
-    halo_start(*p_halo)
-    core_finish(0)
-
-    acc[...] = jnp.zeros((9 * C, 3 * C), F32)
-
-    def grad_one_rows(zi, dzs):
-        return jnp.concatenate(
-            [
-                pim[zi + 1 - dz, C : 2 * C, NY * (2 - dx) : NY * (2 - dx) + L]
-                for dz in dzs
-                for dx in range(3)
-            ],
-            axis=0,
-        )
-
-    def grad_one(zi, carry):
-        acc[...] += dot_nt(grad_one_rows(zi, range(3)), xim[zi, :, NY : NY + L])
-        return carry
-
-    lax.fori_loop(1, NZ + 1, grad_one, 0)
-    acc[0 : 3 * C] += dot_nt(grad_one_rows(0, (0,)), xim[0, :, NY : NY + L])
-    acc[6 * C : 9 * C] += dot_nt(grad_one_rows(NZ + 1, (2,)), xim[NZ + 1, :, NY : NY + L])
-    pack(1, jnp.zeros((8, NY), F32))
-    core_start(1)
-    xy_finish(0)
-
-    core_finish(1)
-    conv_inner(pim, w1f, gh)
-    z_finish(0)
-    xy_finish(1)
-    halo_wait(*p_halo)
-
-    def face_plane(slot, zi, live):
-        for xb in range(NX):
-            v = hp[slot, :, NY * xb : NY * (xb + 1)].astype(F32)
-            put(pim, zi, NY * (xb + 1), jnp.where(live, v, 0.0))
-
-    face_plane(0, 0, has_down)
-    face_plane(1, NZ + 1, has_up)
-    conv_faces(pim, w1f, gh)
-    z_finish(1)
-
-    def finish(zi, carry):
-        for xb in range(NX):
-            v = gh[zi, :, NY * xb : NY * (xb + 1)]
-            up = gim[zi, C : 2 * C, NY * (xb + 1) : NY * (xb + 2)]
-            tmp[pl.ds(xb, C, stride=NX), :] = v + up.astype(F32)
-        out_ref[:, pl.ds(zi - 1, 1)] = tmp[...].reshape(C, 1, NX, NY).astype(BF16)
-        return carry
-
-    lax.fori_loop(1, NZ + 1, finish, 0)
-    gather_finish(0)
-    gather_finish(1)
-    all_finish(0, g2_ref)
-    gb_ref[...] = total[0, 496:504]
-    all_finish(1, g1_ref)
-    drain(0)
-    drain(1)
+    bias_ref[...] = total[0, 496:497, 0:C]
+    gain_ref[...] = total[0, 497:498, 0:C]
+    copy.wait()
 
 
 def local(features, upstream, weight_one, weight_two, norm_gain, norm_bias):
@@ -468,17 +503,21 @@
     w2 = jnp.transpose(weight_two, (2, 3, 4, 0, 1)).reshape(27, C, C)
     vmem = pl.BlockSpec(memory_space=pltpu.VMEM)
     dma = pltpu.SemaphoreType.DMA
-    out, g1, g2, gb = pl.pallas_call(
+    far = pl.BlockSpec(memory_space=pl.ANY)
+    raw, total = pl.pallas_call(
         kernel,
         out_shape=(
             jax.ShapeDtypeStruct((C, NZ, NX, NY), BF16),
-            jax.ShapeDtypeStruct((27, C, C), F32),
-            jax.ShapeDtypeStruct((27, C, C), F32),
-            jax.ShapeDtypeStruct((8, NY), F32),
+            jax.ShapeDtypeStruct((2, ROWS, NY), F32),
         ),
-        in_specs=[vmem] * 6,
-        out_specs=(vmem,) * 4,
+        in_specs=[far] * 4 + [vmem] * 2,
+        out_specs=(vmem,) * 2,
         scratch_shapes=[
+            pltpu.VMEM((C, NZ, NX, NY), BF16),
+            pltpu.VMEM((C, NZ, NX, NY), BF16),
+            pltpu.VMEM((27, C, C), BF16),
+            pltpu.VMEM((27, C, C), BF16),
+            dma((4,)),
             pltpu.VMEM((NZ + 2, 3 * C, LP), BF16),
             pltpu.VMEM((NZ + 2, 3 * C, LP), BF16),
             pltpu.VMEM((NZ, 3 * C, L), BF16),
@@ -499,7 +538,6 @@
             pltpu.VMEM((2, HALF, NY), F32),
             pltpu.VMEM((2, NXY, PIECE, NY), F32),
             pltpu.VMEM((2, NZZ, PIECE, NY), F32),
-            pltpu.VMEM((2, ROWS, NY), F32),
             dma((3, 2)), dma((3, 2)),
             dma((2, NSP)), dma((2, NSP)),
             dma((2,)), dma((2,)),
@@ -520,10 +558,24 @@
         norm_bias.reshape(1, C),
     )
 
+    out, g1, g2, gain, bias = pl.pallas_call(
+        results,
+        out_shape=(
+            jax.ShapeDtypeStruct((C, NZ, NX, NY), BF16),
+            jax.ShapeDtypeStruct((27, C, C), F32),
+            jax.ShapeDtypeStruct((27, C, C), F32),
+            jax.ShapeDtypeStruct((1, C), F32),
+            jax.ShapeDtypeStruct((1, C), F32),
+        ),
+        in_specs=[far, vmem],
+        out_specs=(vmem,) * 5,
+        scratch_shapes=[pltpu.SemaphoreType.DMA],
+    )(raw, total)
+
     def grad(m):
         return jnp.transpose(m.reshape(3, 3, 3, C, C), (3, 4, 0, 1, 2))
 
-    return out.reshape(1, C, NZ, NX, NY), grad(g1), grad(g2), gb[1, :C], gb[0, :C]
+    return out.reshape(1, C, NZ, NX, NY), grad(g1), grad(g2), gain.reshape(C), bias.reshape(C)
 
 
 def solution(mesh):

time: 73.1 us -> 67.3 us (0.921)
  local copies, waits for them, and re-layouts: 5.58 us -> 0 us
    unnamed x7 -> x0, local copies, waits for them, and re-layouts: 4.3 us -> none
    pallas_call x1, Pallas kernels: 66.6 us -> 62.9 us  [local(): pl.pallas_call(kernel, out_shape=(jax.ShapeDtypeStruct((C, NZ, NX, NY), B...]
    pallas_call x0 -> x1, Pallas kernels: none -> 3.51 us  [local(): pl.pallas_call(results, out_shape=(jax.ShapeDtypeStruct((C, NZ, NX, NY),...]
    squeeze x1 -> x0, local copies, waits for them, and re-layouts: 1.28 us -> none  [local(): gb[0, :C]]
where the time goes in v2:
time: 67.3 us; the launch traced here: 67.1 us
  Pallas kernels  66.4 us (99%)
    pallas_call x1, Pallas kernels, local(): pl.pallas_call(kernel, out_shape=(jax.ShapeDtypeStruct((C, NZ, NX, NY), B...  62.9 us
    pallas_call x1, Pallas kernels, local(): pl.pallas_call(results, out_shape=(jax.ShapeDtypeStruct((C, NZ, NX, NY),...  3.51 us

profile of v2, /device:TPU:1, one launch (start us, length us, event | category | flops | bytes accessed | tf_op | source)
XLA Modules:
  0.0 67.1 jit_solution(6041246898287417410)
XLA Ops:
  0.6 62.9 %shard_map.101 = (bf16[48,8,8,128]{3,2,1,0:T(8,128)(2,1)}, f32[2,512,128]{2,1,0:T(8,128)}) custom-call(bf16[48,8,8,128]{3,2,1,0:T(8,128)(2,1)} %bitcast.19, bf16[48,8,8,128]{3,2,1,0:T(8,128)(2,1)} %bitcast.20, bf16[27,48,48]{2,1,0:T(8,128)(2,1)} %bitcast.21, bf16[27,48,48]{2,1,0:T(8,128)(2,1)} %bitcast.22, f32[1,48]{1,0:T(1,128)} %bitcast.23, f32[1,48]{1,0:T(1,128)} %bitcast.24), custom_call_target="tpu_custom_call" | custom-call | tf_op jit(solution)/shard_map/pallas_call | solution.py:507
  63.6 3.5 %shard_map.102 = (bf16[48,8,8,128]{3,2,1,0:T(8,128)(2,1)}, f32[27,48,48]{2,1,0:T(8,128)}, f32[27,48,48]{2,1,0:T(8,128)}, f32[1,48]{1,0:T(1,128)}, f32[1,48]{1,0:T(1,128)}) custom-call(bf16[48,8,8,128]{3,2,1,0:T(8,128)(2,1)} %get-tuple-element.12.raw, f32[2,512,128]{2,1,0:T(8,128)} %get-tuple-element.13.total), custom_call_target="tpu_custom_call" | custom-call | tf_op jit(solution)/shard_map/pallas_call | solution.py:561

commit v3 on v2

--- a/solution.py
+++ b/solution.py
@@ -34,9 +34,9 @@
 
 
 def kernel(
-    x_hbm, g_hbm, w1_hbm, w2_hbm, gain_ref, bias_ref,
-    out_ref, total,
-    x_ref, g_ref, w1_ref, w2_ref, load,
+    x_hbm, g_hbm, w1_hbm, w2_hbm, gain_hbm, bias_hbm,
+    out_ref, total, g2_ref,
+    x_ref, g_ref, w1_ref, w2_ref, gain_ref, bias_ref, load,
     xim, gim, him, pim, pre, gh, tmp, hx, hg, hp, w1c, w2f, w1f,
     st, acc, part, core_in, half_sum, xy_in, z_in,
     halo_send, halo_recv, st_send, st_recv, c_send, c_recv, xy_send, xy_recv, z_send, z_recv,
@@ -65,10 +65,26 @@
             return carry
         lax.fori_loop(1, count, step, 0)
 
+    ys = [(y + o) % SY for o in range(SY)]
+    xs = [(xx_ + o) % SX for o in range(SX)]
+    hops = (0, 1, 2, 1)
+    offsets = sorted(((a, b) for a in range(SX) for b in range(SY)), key=lambda o: -hops[o[0]] - hops[o[1]])
+    xy_peers = [
+        (xs[a] * SY + ys[b], (z_hi * SY + ys[b], xs[a] * (SZ_LO * 2) + z_lo * 2 + core))
+        for a, b in offsets[:-1]
+    ]
+    sp_peers = [
+        (side * SY + ys[b], (side * SY + ys[b], dp))
+        for side, bs in ((1 - z_hi, (2, 1, 3, 0)), (z_hi, (2, 1, 3)))
+        for b in bs
+    ]
+    z_ids = [(me_z + o) % NZZ for o in (4, 3, 5, 2, 6, 1, 7)]
+    z_peers = [(j, z_dev(j)) for j in z_ids]
+
     loads = [
         pltpu.make_async_copy(src, dst, load.at[i])
         for i, (src, dst) in enumerate(
-            ((x_hbm, x_ref), (w1_hbm, w1_ref), (w2_hbm, w2_ref), (g_hbm, g_ref))
+            ((x_hbm, x_ref), (w1_hbm, w1_ref), (w2_hbm, w2_ref), (g_hbm, g_ref), (gain_hbm, gain_ref), (bias_hbm, bias_ref))
         )
     ]
     for each in loads:
@@ -79,10 +95,9 @@
     def greet(dev):
         pl.semaphore_signal(barrier, inc=1, device_id=dev, device_id_type=MESH)
 
+    for _, dev in sp_peers + z_peers + xy_peers:
+        greet(dev)
     greet(sibling)
-    others(NSP, sp, lambda j: greet(sp_dev(j)))
-    others(NXY, me_xy, lambda j: greet(xy_dev(j)))
-    others(NZZ, me_z, lambda j: greet(z_dev(j)))
 
     lane = lax.broadcasted_iota(jnp.int32, (C, NY), 1)
     eye = lax.broadcasted_iota(jnp.int32, (C, NY), 0) == lane
@@ -111,11 +126,8 @@
             return carry
         lax.fori_loop(begin, begin + NZ, step, 0)
 
-    def unpack(raw, im, zi, live):
-        plane = raw.astype(F32)
-        if live is not None:
-            plane = jnp.where(live, plane, 0.0)
-        tmp[...] = plane.reshape(C * NX, NY)
+    def unpack(raw, im, zi):
+        tmp[...] = raw.astype(F32).reshape(C * NX, NY)
         for xb in range(NX):
             put(im, zi, NY * (xb + 1), tmp[pl.ds(xb, C, stride=NX), :])
 
@@ -133,7 +145,7 @@
 
     def unpack_own(src, im):
         def step(zi, carry):
-            unpack(src[:, pl.ds(zi, 1)].reshape(C, NX, NY), im, zi + 1, None)
+            unpack(src[:, pl.ds(zi, 1)].reshape(C, NX, NY), im, zi + 1)
             return carry
         lax.fori_loop(0, NZ, step, 0)
 
@@ -178,8 +190,13 @@
             halo_copy(low, dst, k, 1, (sp - 1, dp)).wait_send()
             halo_copy(low, dst, k, 0, (sp - 1, dp)).wait_recv()
 
-    x_halo = (x_ref.at[:, 0], x_ref.at[:, NZ - 1], hx, 0)
-    g_halo = (g_ref.at[:, 0], g_ref.at[:, NZ - 1], hg, 1)
+    def halo_of(im, dst, k):
+        at = (slice(C, 2 * C), slice(NY, NY + L))
+        return im.at[(1,) + at], im.at[(NZ,) + at], dst, k
+
+    x_halo = halo_of(xim, hx, 0)
+    g_halo = halo_of(gim, hg, 1)
+    p_halo = halo_of(pim, hp, 2)
 
     def window(im, zi):
         return jnp.concatenate([im[zi, :, NY * d : NY * d + L] for d in range(3)], axis=0)
@@ -202,13 +219,15 @@
         dst[NZ] += dot(w[2 * C : 3 * C], window(im, NZ + 1))
 
     def face_planes(dst, im):
-        unpack(dst[0], im, 0, has_down)
-        unpack(dst[1], im, NZ + 1, has_up)
-
-    def st_copy(k, j):
+        for slot, zi, live in ((0, 0, has_down), (1, NZ + 1, has_up)):
+            for xb in range(NX):
+                v = dst[slot, :, NY * xb : NY * (xb + 1)].astype(F32)
+                put(im, zi, NY * (xb + 1), jnp.where(live, v, 0.0))
+
+    def st_copy(k, j, dev):
         return pltpu.make_async_remote_copy(
             src_ref=st.at[k, sp], dst_ref=st.at[k, sp], send_sem=st_send.at[k, j],
-            recv_sem=st_recv.at[k, sp], device_id=sp_dev(j), device_id_type=MESH,
+            recv_sem=st_recv.at[k, sp], device_id=dev, device_id_type=MESH,
         )
 
     def st_wait(k, j):
@@ -223,12 +242,12 @@
         lead = lax.broadcasted_iota(jnp.int32, (8, NY), 0)
         mine = jnp.where(lead == 0, row_one, 0.0) + jnp.where(lead == 1, row_two, 0.0)
         st[k, sp] = mine
-        others(NSP, sp, lambda j: st_copy(k, j).start())
+        for j, dev in sp_peers:
+            st_copy(k, j, dev).start()
         return mine
 
     def st_finish(k):
         others(NSP, sp, lambda j: st_wait(k, j).wait_recv())
-        others(NSP, sp, lambda j: st_copy(k, j).wait_send())
         s = st[k, 0]
         for j in range(1, NSP):
             s = s + st[k, j]
@@ -242,9 +261,6 @@
     halo_start(*x_halo)
     halo_start(*g_halo)
     conv_inner(gim, w2f, gh)
-    halo_wait(*x_halo)
-    face_planes(hx, xim)
-    conv_faces(xim, w1c, pre)
 
     zero = jnp.zeros((C, NY), F32)
 
@@ -255,12 +271,18 @@
             one, two = one + v, two + v * v
         return one, two
 
-    st_start(0, *lax.fori_loop(1, NZ + 1, moments, (zero, zero)))
+    sums = lax.fori_loop(2, NZ, moments, (zero, zero))
+    halo_wait(*x_halo)
+    face_planes(hx, xim)
+    conv_faces(xim, w1c, pre)
+    st_start(0, *moments(NZ, moments(1, sums)))
 
     halo_wait(*g_halo)
     face_planes(hg, gim)
     conv_faces(gim, w2f, gh)
 
+    loads[4].wait()
+    loads[5].wait()
     pad = jnp.zeros((1, NY - C), F32)
     gain = column(jnp.concatenate([gain_ref[...], pad], axis=1))
     bias = column(jnp.concatenate([bias_ref[...], pad], axis=1))
@@ -303,10 +325,10 @@
     def core_start(k):
         c_copy(k).start()
 
-    def xy_copy(k, j):
+    def xy_copy(k, j, dev):
         return pltpu.make_async_remote_copy(
             src_ref=half_sum.at[k, pl.ds(j * PIECE, PIECE)], dst_ref=xy_in.at[k, me_xy],
-            send_sem=xy_send.at[k, j], recv_sem=xy_recv.at[k, me_xy], device_id=xy_dev(j), device_id_type=MESH,
+            send_sem=xy_send.at[k, j], recv_sem=xy_recv.at[k, me_xy], device_id=dev, device_id_type=MESH,
         )
 
     def xy_wait(k, j):
@@ -316,14 +338,15 @@
         )
 
     def core_finish(k):
-        c_copy(k).wait()
+        c_copy(k).wait_recv()
         half_sum[k] = part[k, pl.ds(core * HALF, HALF)] + core_in[k]
-        others(NXY, me_xy, lambda j: xy_copy(k, j).start())
-
-    def z_copy(k, j):
+        for j, dev in xy_peers:
+            xy_copy(k, j, dev).start()
+
+    def z_copy(k, j, dev):
         return pltpu.make_async_remote_copy(
             src_ref=z_in.at[k, me_z], dst_ref=z_in.at[k, me_z],
-            send_sem=z_send.at[k, j], recv_sem=z_recv.at[k, me_z], device_id=z_dev(j), device_id_type=MESH,
+            send_sem=z_send.at[k, j], recv_sem=z_recv.at[k, me_z], device_id=dev, device_id_type=MESH,
         )
 
     def z_wait(k, j):
@@ -339,15 +362,16 @@
         for j in range(1, NXY):
             s = s + xy_in[k, j]
         z_in[k, me_z] = s
-        others(NZZ, me_z, lambda j: z_copy(k, j).start())
+        for j, dev in z_peers:
+            z_copy(k, j, dev).start()
 
     def ga_at(j):
         return pl.ds(core * HALF + j * PIECE, PIECE)
 
-    def ga_copy(k, j):
+    def ga_copy(k, j, dev):
         return pltpu.make_async_remote_copy(
             src_ref=total.at[k, ga_at(me_xy)], dst_ref=total.at[k, ga_at(me_xy)],
-            send_sem=ga_send.at[k, j], recv_sem=ga_recv.at[k, me_xy], device_id=xy_dev(j), device_id_type=MESH,
+            send_sem=ga_send.at[k, j], recv_sem=ga_recv.at[k, me_xy], device_id=dev, device_id_type=MESH,
         )
 
     def ga_wait(k, j):
@@ -362,7 +386,8 @@
         for j in range(1, NZZ):
             s = s + z_in[k, j]
         total[k, ga_at(me_xy)] = s
-        others(NXY, me_xy, lambda j: ga_copy(k, j).start())
+        for j, dev in xy_peers:
+            ga_copy(k, j, dev).start()
 
     def cg_copy(k, which):
         at = pl.ds(which * HALF, HALF)
@@ -376,9 +401,11 @@
         cg_copy(k, core).start()
 
     def drain(k):
-        others(NXY, me_xy, lambda j: xy_copy(k, j).wait_send())
-        others(NXY, me_xy, lambda j: ga_copy(k, j).wait_send())
-        others(NZZ, me_z, lambda j: z_copy(k, j).wait_send())
+        others(NSP, sp, lambda j: st_copy(k, j, sp_dev(j)).wait_send())
+        others(NXY, me_xy, lambda j: xy_copy(k, j, xy_dev(j)).wait_send())
+        others(NXY, me_xy, lambda j: ga_copy(k, j, xy_dev(j)).wait_send())
+        others(NZZ, me_z, lambda j: z_copy(k, j, z_dev(j)).wait_send())
+        c_copy(k).wait_send()
 
     def all_finish(k):
         cg_copy(k, core).wait_send()
@@ -421,7 +448,6 @@
         return carry
 
     lax.fori_loop(1, NZ + 1, before, 0)
-    p_halo = (pim.at[1, C : 2 * C, NY : NY + L], pim.at[NZ, C : 2 * C, NY : NY + L], hp, 2)
     halo_start(*p_halo)
 
     acc[...] = jnp.zeros((9 * C, 3 * C), F32)
@@ -445,13 +471,7 @@
     xy_finish(1)
     halo_wait(*p_halo)
 
-    def face_plane(slot, zi, live):
-        for xb in range(NX):
-            v = hp[slot, :, NY * xb : NY * (xb + 1)].astype(F32)
-            put(pim, zi, NY * (xb + 1), jnp.where(live, v, 0.0))
-
-    face_plane(0, 0, has_down)
-    face_plane(1, NZ + 1, has_up)
+    face_planes(hp, pim)
     conv_faces(pim, w1f, gh)
 
     def finish(zi, carry):
@@ -466,36 +486,47 @@
     z_finish(0)
     z_finish(1)
     gather_finish(0)
+    all_finish(0)
+    separate(total, 0, g2_ref)
     gather_finish(1)
-    all_finish(0)
     all_finish(1)
     drain(0)
     drain(1)
 
 
+def separate(total, k, dst):
+    for b in range(9):
+        m = total[k, b * C : (b + 1) * C]
+        dst[3 * b] = m[:, 0:C]
+        dst[3 * b + 1] = m[:, C : 2 * C]
+        r, o = (b * C) // 64, (b * C) % 64
+        rows = []
+        left = C
+        while left:
+            n = min(64 - o, left)
+            rows.append(total[k, 9 * C + o : 9 * C + o + n, 16 * r : 16 * (r + 1)])
+            left -= n
+            r, o = r + 1, 0
+        tail = rows[0] if len(rows) == 1 else jnp.concatenate(rows, axis=0)
+        dst[3 * b + 2] = jnp.concatenate([m[:, 2 * C : NY], tail], axis=1)
+
+
 def results(
-    raw, total, out_ref, g1_ref, g2_ref, gain_ref, bias_ref, sem
+    raw, total, g2_raw, out_ref, g1_ref, g2_ref, gain_ref, bias_ref, g1, gain, bias, sem
 ):
-    copy = pltpu.make_async_copy(raw, out_ref, sem)
-    copy.start()
-    for k, dst in ((0, g2_ref), (1, g1_ref)):
-        for b in range(9):
-            m = total[k, b * C : (b + 1) * C]
-            dst[3 * b] = m[:, 0:C]
-            dst[3 * b + 1] = m[:, C : 2 * C]
-            r, o = (b * C) // 64, (b * C) % 64
-            rows = []
-            left = C
-            while left:
-                n = min(64 - o, left)
-                rows.append(total[k, 9 * C + o : 9 * C + o + n, 16 * r : 16 * (r + 1)])
-                left -= n
-                r, o = r + 1, 0
-            tail = rows[0] if len(rows) == 1 else jnp.concatenate(rows, axis=0)
-            dst[3 * b + 2] = jnp.concatenate([m[:, 2 * C : NY], tail], axis=1)
-    bias_ref[...] = total[0, 496:497, 0:C]
-    gain_ref[...] = total[0, 497:498, 0:C]
-    copy.wait()
+    def copy(i, src, dst):
+        each = pltpu.make_async_copy(src, dst, sem.at[i])
+        each.start()
+        return each
+
+    copies = [copy(0, raw, out_ref), copy(1, g2_raw, g2_ref)]
+    bias[...] = total[0, 496:497, 0:C]
+    gain[...] = total[0, 497:498, 0:C]
+    copies += [copy(2, gain, gain_ref), copy(3, bias, bias_ref)]
+    separate(total, 1, g1)
+    copies.append(copy(4, g1, g1_ref))
+    for each in copies:
+        each.wait()
 
 
 def local(features, upstream, weight_one, weight_two, norm_gain, norm_bias):
@@ -503,21 +534,24 @@
     w2 = jnp.transpose(weight_two, (2, 3, 4, 0, 1)).reshape(27, C, C)
     vmem = pl.BlockSpec(memory_space=pltpu.VMEM)
     dma = pltpu.SemaphoreType.DMA
-    far = pl.BlockSpec(memory_space=pl.ANY)
-    raw, total = pl.pallas_call(
+    far = pl.BlockSpec(memory_space=pltpu.HBM)
+    raw, total, g2_raw = pl.pallas_call(
         kernel,
         out_shape=(
-            jax.ShapeDtypeStruct((C, NZ, NX, NY), BF16),
-            jax.ShapeDtypeStruct((2, ROWS, NY), F32),
+            pltpu.VMEM((C, NZ, NX, NY), BF16),
+            pltpu.VMEM((2, ROWS, NY), F32),
+            pltpu.VMEM((27, C, C), F32),
         ),
-        in_specs=[far] * 4 + [vmem] * 2,
-        out_specs=(vmem,) * 2,
+        in_specs=[far] * 6,
+        out_specs=(vmem,) * 3,
         scratch_shapes=[
             pltpu.VMEM((C, NZ, NX, NY), BF16),
             pltpu.VMEM((C, NZ, NX, NY), BF16),
             pltpu.VMEM((27, C, C), BF16),
             pltpu.VMEM((27, C, C), BF16),
-            dma((4,)),
+            pltpu.VMEM((1, C), F32),
+            pltpu.VMEM((1, C), F32),
+            dma((6,)),
             pltpu.VMEM((NZ + 2, 3 * C, LP), BF16),
             pltpu.VMEM((NZ + 2, 3 * C, LP), BF16),
             pltpu.VMEM((NZ, 3 * C, L), BF16),
@@ -525,8 +559,8 @@
             pltpu.VMEM((NZ + 2, C, L), F32),
             pltpu.VMEM((NZ + 2, C, L), F32),
             pltpu.VMEM((C * NX, NY), F32),
-            pltpu.VMEM((2, C, NX, NY), BF16),
-            pltpu.VMEM((2, C, NX, NY), BF16),
+            pltpu.VMEM((2, C, L), BF16),
+            pltpu.VMEM((2, C, L), BF16),
             pltpu.VMEM((2, C, L), BF16),
             pltpu.VMEM((3 * C, 9 * C), BF16),
             pltpu.VMEM((3 * C, 9 * C), BF16),
@@ -567,10 +601,15 @@
             jax.ShapeDtypeStruct((1, C), F32),
             jax.ShapeDtypeStruct((1, C), F32),
         ),
-        in_specs=[far, vmem],
-        out_specs=(vmem,) * 5,
-        scratch_shapes=[pltpu.SemaphoreType.DMA],
-    )(raw, total)
+        in_specs=[vmem] * 3,
+        out_specs=(far,) * 5,
+        scratch_shapes=[
+            pltpu.VMEM((27, C, C), F32),
+            pltpu.VMEM((1, C), F32),
+            pltpu.VMEM((1, C), F32),
+            dma((5,)),
+        ],
+    )(*(pltpu.with_memory_space_constraint(v, pltpu.VMEM) for v in (raw, total, g2_raw)))
 
     def grad(m):
         return jnp.transpose(m.reshape(3, 3, 3, C, C), (3, 4, 0, 1, 2))

time: 67.3 us -> 62.7 us (0.932)
  Pallas kernels: 66.4 us -> 62 us
    pallas_call x1, Pallas kernels: 62.9 us -> 60.6 us  [local(): pl.pallas_call(kernel, out_shape=(pltpu.VMEM((C, NZ, NX, NY), BF16), pltp...]
    pallas_call x1, Pallas kernels: 3.51 us -> 1.37 us  [local(): pl.pallas_call(results, out_shape=(jax.ShapeDtypeStruct((C, NZ, NX, NY),...]
where the time goes in v3:
time: 62.7 us; the launch traced here: 62.6 us
  Pallas kernels  62 us (99%)
  between operations  0.64 us (1%)
    pallas_call x1, Pallas kernels, local(): pl.pallas_call(kernel, out_shape=(pltpu.VMEM((C, NZ, NX, NY), BF16), pltp...  60.6 us
    pallas_call x1, Pallas kernels, local(): pl.pallas_call(results, out_shape=(jax.ShapeDtypeStruct((C, NZ, NX, NY),...  1.37 us

profile of v3, /device:TPU:1, one launch (start us, length us, event | category | flops | bytes accessed | tf_op | source)
XLA Modules:
  0.0 62.6 jit_solution(17532947827151219285)
XLA Ops:
  0.6 60.6 %shard_map.101 = (bf16[48,8,8,128]{3,2,1,0:T(8,128)(2,1)S(1)}, f32[2,512,128]{2,1,0:T(8,128)S(1)}, f32[27,48,48]{2,1,0:T(8,128)S(1)}) custom-call(bf16[48,8,8,128]{3,2,1,0:T(8,128)(2,1)} %bitcast.19, bf16[48,8,8,128]{3,2,1,0:T(8,128)(2,1)} %bitcast.20, bf16[27,48,48]{2,1,0:T(8,128)(2,1)} %bitcast.21, bf16[27,48,48]{2,1,0:T(8,128)(2,1)} %bitcast.22, ...), custom_call_target="tpu_custom_call" | custom-call | tf_op jit(solution)/shard_map/pallas_call | solution.py:538
  61.3 1.4 %shard_map.102 = (bf16[48,8,8,128]{3,2,1,0:T(8,128)(2,1)}, f32[27,48,48]{2,1,0:T(8,128)}, f32[27,48,48]{2,1,0:T(8,128)}, f32[1,48]{1,0:T(1,128)}, f32[1,48]{1,0:T(1,128)}) custom-call(bf16[48,8,8,128]{3,2,1,0:T(8,128)(2,1)S(1)} %get-tuple-element.13.raw, f32[2,512,128]{2,1,0:T(8,128)S(1)} %get-tuple-element.14.total, f32[27,48,48]{2,1,0:T(8,128)S(1)} %get-tuple-element.15.g2_raw), custom_call_target="tpu_custom_call" | custom-call | tf_op jit(solution)/shard_map/pallas_call | solution.py:595

commit v4 on v3

--- a/solution.py
+++ b/solution.py
@@ -23,6 +23,7 @@
 ROWS = 512
 HALF = ROWS // 2
 PIECE = HALF // NXY
+SPLIT = 9 * C // 2
 
 
 def dot(a, b):
@@ -38,7 +39,7 @@
     out_ref, total, g2_ref,
     x_ref, g_ref, w1_ref, w2_ref, gain_ref, bias_ref, load,
     xim, gim, him, pim, pre, gh, tmp, hx, hg, hp, w1c, w2f, w1f,
-    st, acc, part, core_in, half_sum, xy_in, z_in,
+    st, cols, acc, part, core_in, half_sum, xy_in, z_in,
     halo_send, halo_recv, st_send, st_recv, c_send, c_recv, xy_send, xy_recv, z_send, z_recv,
     ga_send, ga_recv, cg_send, cg_recv,
 ):
@@ -254,11 +255,11 @@
         return column(s[0:1] / CELLS), column(s[1:2] / CELLS)
 
     conv_inner(xim, w1c, pre)
+    pl.semaphore_wait(barrier, 1 + (NSP - 1) + (NXY - 1) + (NZZ - 1))
+
+    halo_start(*x_halo)
     loads[3].wait()
     unpack_own(g_ref, gim)
-    pl.semaphore_wait(barrier, 1 + (NSP - 1) + (NXY - 1) + (NZZ - 1))
-
-    halo_start(*x_halo)
     halo_start(*g_halo)
     conv_inner(gim, w2f, gh)
 
@@ -284,20 +285,27 @@
     loads[4].wait()
     loads[5].wait()
     pad = jnp.zeros((1, NY - C), F32)
+    def spread(i, col):
+        cols[i] = jnp.broadcast_to(col, (C, NY))
+
     gain = column(jnp.concatenate([gain_ref[...], pad], axis=1))
-    bias = column(jnp.concatenate([bias_ref[...], pad], axis=1))
+    spread(2, gain)
+    spread(3, column(jnp.concatenate([bias_ref[...], pad], axis=1)))
     mean, square = st_finish(0)
     inv_std = lax.rsqrt(square - mean * mean + EPS)
+    spread(0, mean)
+    spread(1, inv_std)
 
     def activate(zi, carry):
         one, two = carry
         for xb in range(NX):
             at = slice(NY * xb, NY * (xb + 1))
-            hat = (pre[zi, :, at] - mean) * inv_std
-            normed = hat * gain + bias
+            hat = (pre[zi, :, at] - cols[0]) * cols[1]
+            normed = hat * cols[2] + cols[3]
             sig = jax.nn.sigmoid(normed)
-            him[zi - 1, C : 2 * C, at] = (normed * sig).astype(BF16)
-            gn = gh[zi, :, at] * sig * (1.0 + normed * (1.0 - sig))
+            act = normed * sig
+            him[zi - 1, C : 2 * C, at] = act.astype(BF16)
+            gn = gh[zi, :, at] * (sig + act * (1.0 - sig))
             gh[zi, :, at] = gn
             pre[zi, :, at] = hat
             one, two = one + gn, two + gn * hat
@@ -311,16 +319,13 @@
             send_sem=c_send.at[k], recv_sem=c_recv.at[k], device_id=sibling, device_id_type=MESH,
         )
 
-    def pack(k, tail):
-        main = acc[:, 0:NY]
-        part[k, 0 : 9 * C] = main
-        rest = acc[:, NY : NY + 16]
-        pieces = [rest[64 * r : 64 * (r + 1)] for r in range(6)]
-        pieces.append(jnp.concatenate([rest[384:432], jnp.zeros((16, 16), F32)], axis=0))
-        pieces.append(jnp.zeros((64, 16), F32))
-        part[k, 9 * C : 9 * C + 64] = jnp.concatenate(pieces, axis=1)
-        part[k, 496:504] = tail
-        part[k, 504:512] = jnp.zeros((8, NY), F32)
+    def pack(k, p, v, tail):
+        base = p * HALF
+        part[k, pl.ds(base, SPLIT)] = v[:, 0:NY]
+        rest = jnp.concatenate([v[:, NY : NY + 16], jnp.zeros((256 - SPLIT, 16), F32)], axis=0)
+        pieces = [rest[32 * r : 32 * (r + 1)] for r in range(8)]
+        part[k, pl.ds(base + SPLIT, 32)] = jnp.concatenate(pieces, axis=1)
+        part[k, pl.ds(base + SPLIT + 32, 8)] = tail
 
     def core_start(k):
         c_copy(k).start()
@@ -386,19 +391,21 @@
         for j in range(1, NZZ):
             s = s + z_in[k, j]
         total[k, ga_at(me_xy)] = s
+        cg_copy(k, core, me_xy).start()
         for j, dev in xy_peers:
             ga_copy(k, j, dev).start()
 
-    def cg_copy(k, which):
-        at = pl.ds(which * HALF, HALF)
+    def cg_copy(k, which, j):
+        at = pl.ds(which * HALF + j * PIECE, PIECE)
         return pltpu.make_async_remote_copy(
             src_ref=total.at[k, at], dst_ref=total.at[k, at],
-            send_sem=cg_send.at[k], recv_sem=cg_recv.at[k], device_id=sibling, device_id_type=MESH,
+            send_sem=cg_send.at[k, j], recv_sem=cg_recv.at[k, j], device_id=sibling, device_id_type=MESH,
         )
 
     def gather_finish(k):
-        others(NXY, me_xy, lambda j: ga_wait(k, j).wait_recv())
-        cg_copy(k, core).start()
+        for j, _ in reversed(xy_peers):
+            ga_wait(k, j).wait_recv()
+            cg_copy(k, core, j).start()
 
     def drain(k):
         others(NSP, sp, lambda j: st_copy(k, j, sp_dev(j)).wait_send())
@@ -406,68 +413,88 @@
         others(NXY, me_xy, lambda j: ga_copy(k, j, xy_dev(j)).wait_send())
         others(NZZ, me_z, lambda j: z_copy(k, j, z_dev(j)).wait_send())
         c_copy(k).wait_send()
+        all_sent(k)
 
     def all_finish(k):
-        cg_copy(k, core).wait_send()
-        cg_copy(k, 1 - core).wait_recv()
+        def step(j, carry):
+            cg_copy(k, 1 - core, j).wait_recv()
+            return carry
+        lax.fori_loop(0, NXY, step, 0)
+
+    def all_sent(k):
+        def step(j, carry):
+            cg_copy(k, core, j).wait_send()
+            return carry
+        lax.fori_loop(0, NXY, step, 0)
 
     sides(him, 0, 0)
-    acc[...] = jnp.zeros((9 * C, 3 * C), F32)
-
-    def shifted(im, zi, dzs):
-        return jnp.concatenate(
-            [
-                im[zi + 1 - dz, C : 2 * C, NY * (2 - dx) : NY * (2 - dx) + L]
-                for dz in dzs
-                for dx in range(3)
-            ],
-            axis=0,
-        )
-
-    def pair(im, zi):
-        return jnp.concatenate([shifted(im, zi, range(3)), shifted(im, zi + 1, range(3))], axis=1)
-
-    def grad_two(i, carry):
-        zi = 2 * i
-        acc[...] += dot_nt(pair(gim, zi + 1), jnp.concatenate([him[zi], him[zi + 1]], axis=1))
-        return carry
-
-    lax.fori_loop(0, NZ // 2, grad_two, 0)
-    pack(0, slopes)
+    lhs = jnp.concatenate(
+        [
+            jnp.concatenate(
+                [
+                    gim[zi + 1 - dz, C : 2 * C, NY * (2 - dx) : NY * (2 - dx) + L]
+                    for dz in range(3)
+                    for dx in range(3)
+                ],
+                axis=0,
+            )
+            for zi in range(1, NZ + 1)
+        ],
+        axis=1,
+    )
+    acc[...] = dot_nt(lhs, jnp.concatenate([him[zi] for zi in range(NZ)], axis=1))
+    pack(0, 0, acc[0:SPLIT], slopes)
+    pack(0, 1, acc[SPLIT : 2 * SPLIT], jnp.zeros((8, NY), F32))
     core_start(0)
+    core_finish(0)
 
     slope, slope_dot = st_finish(1)
-    core_finish(0)
-    scale = gain * inv_std
+    spread(4, gain * inv_std)
+    spread(5, slope)
+    spread(6, slope_dot)
 
     def before(zi, carry):
         for xb in range(NX):
             at = slice(NY * xb, NY * (xb + 1))
-            gp = scale * (gh[zi, :, at] - slope - pre[zi, :, at] * slope_dot)
+            gp = cols[4] * (gh[zi, :, at] - cols[5] - pre[zi, :, at] * cols[6])
             pim[zi, C : 2 * C, NY * (xb + 1) : NY * (xb + 2)] = gp.astype(BF16)
         return carry
 
     lax.fori_loop(1, NZ + 1, before, 0)
     halo_start(*p_halo)
 
-    acc[...] = jnp.zeros((9 * C, 3 * C), F32)
-
-    def grad_one(i, carry):
-        zi = 2 * i + 1
-        at = slice(NY, NY + L)
-        acc[...] += dot_nt(pair(pim, zi), jnp.concatenate([xim[zi, :, at], xim[zi + 1, :, at]], axis=1))
-        return carry
-
-    lax.fori_loop(0, NZ // 2, grad_one, 0)
-    acc[0 : 3 * C] += dot_nt(shifted(pim, 0, (0,)), xim[0, :, NY : NY + L])
-    acc[6 * C : 9 * C] += dot_nt(shifted(pim, NZ + 1, (2,)), xim[NZ + 1, :, NY : NY + L])
-    pack(1, jnp.zeros((8, NY), F32))
+    def grad_one(p):
+        def block(zi, i):
+            b = 4 * p + i
+            dz, dx = b // 3, b % 3
+            return pim[zi + 1 - dz, C : 2 * C, pl.ds(pl.multiple_of(NY * (2 - dx), NY), L)]
+
+        lhs = jnp.concatenate(
+            [
+                jnp.concatenate([block(zi, i) for i in range(5)], axis=0)
+                for zi in range(1, NZ + 1)
+            ],
+            axis=1,
+        )
+        inner = slice(NY, NY + L)
+        rhs = jnp.concatenate([xim[zi, :, inner] for zi in range(1, NZ + 1)], axis=1)
+        acc[0 : 5 * C] = dot_nt(lhs, rhs)
+        face = jnp.concatenate(
+            [pim[1 + (NZ - 1) * p, C : 2 * C, NY * (2 - dx) : NY * (2 - dx) + L] for dx in range(3)], axis=0
+        )
+        rows = pl.ds(pl.multiple_of(2 * C * p, 8), 3 * C)
+        acc[rows] += dot_nt(face, xim[(NZ + 1) * p, :, inner])
+        pack(1, p, acc[pl.ds(pl.multiple_of((C // 2) * p, 8), SPLIT)], jnp.zeros((8, NY), F32))
+
+    grad_one(1 - core)
     core_start(1)
-
+    grad_one(core)
+    core_finish(1)
+
+    xy_finish(0)
     sides(pim, 1, NY)
-    core_finish(1)
     conv_inner(pim, w1f, gh)
-    xy_finish(0)
+    z_finish(0)
     xy_finish(1)
     halo_wait(*p_halo)
 
@@ -483,32 +510,33 @@
         return carry
 
     lax.fori_loop(1, NZ + 1, finish, 0)
-    z_finish(0)
+    gather_finish(0)
     z_finish(1)
-    gather_finish(0)
     all_finish(0)
     separate(total, 0, g2_ref)
     gather_finish(1)
+    drain(0)
     all_finish(1)
-    drain(0)
     drain(1)
 
 
-def separate(total, k, dst):
+def separate(total, k, dst, done=None):
+    main, tail = [], []
+    for p in range(2):
+        base = p * HALF
+        rest = [total[k, base + SPLIT : base + SPLIT + 32, 16 * r : 16 * (r + 1)] for r in range(7)]
+        rest[6] = rest[6][0 : SPLIT - 192]
+        main.append(total[k, base : base + SPLIT])
+        tail.append(jnp.concatenate(rest, axis=0))
+    main, tail = jnp.concatenate(main, axis=0), jnp.concatenate(tail, axis=0)
     for b in range(9):
-        m = total[k, b * C : (b + 1) * C]
+        rows = slice(b * C, (b + 1) * C)
+        m = main[rows]
         dst[3 * b] = m[:, 0:C]
         dst[3 * b + 1] = m[:, C : 2 * C]
-        r, o = (b * C) // 64, (b * C) % 64
-        rows = []
-        left = C
-        while left:
-            n = min(64 - o, left)
-            rows.append(total[k, 9 * C + o : 9 * C + o + n, 16 * r : 16 * (r + 1)])
-            left -= n
-            r, o = r + 1, 0
-        tail = rows[0] if len(rows) == 1 else jnp.concatenate(rows, axis=0)
-        dst[3 * b + 2] = jnp.concatenate([m[:, 2 * C : NY], tail], axis=1)
+        dst[3 * b + 2] = jnp.concatenate([m[:, 2 * C : NY], tail[rows]], axis=1)
+        if done is not None and b % 3 == 2:
+            done(b // 3)
 
 
 def results(
@@ -520,11 +548,16 @@
         return each
 
     copies = [copy(0, raw, out_ref), copy(1, g2_raw, g2_ref)]
-    bias[...] = total[0, 496:497, 0:C]
-    gain[...] = total[0, 497:498, 0:C]
+    row = SPLIT + 32
+    bias[...] = total[0, row : row + 1, 0:C]
+    gain[...] = total[0, row + 1 : row + 2, 0:C]
     copies += [copy(2, gain, gain_ref), copy(3, bias, bias_ref)]
-    separate(total, 1, g1)
-    copies.append(copy(4, g1, g1_ref))
+
+    def send(third):
+        at = pl.ds(9 * third, 9)
+        copies.append(copy(4 + third, g1.at[at], g1_ref.at[at]))
+
+    separate(total, 1, g1, send)
     for each in copies:
         each.wait()
 
@@ -566,6 +599,7 @@
             pltpu.VMEM((3 * C, 9 * C), BF16),
             pltpu.VMEM((3 * C, 9 * C), BF16),
             pltpu.VMEM((2, NSP, 8, NY), F32),
+            pltpu.VMEM((7, C, NY), F32),
             pltpu.VMEM((9 * C, 3 * C), F32),
             pltpu.VMEM((2, ROWS, NY), F32),
             pltpu.VMEM((2, HALF, NY), F32),
@@ -578,7 +612,7 @@
             dma((2, NXY)), dma((2, NXY)),
             dma((2, NZZ)), dma((2, NZZ)),
             dma((2, NXY)), dma((2, NXY)),
-            dma((2,)), dma((2,)),
+            dma((2, NXY)), dma((2, NXY)),
         ],
         compiler_params=pltpu.CompilerParams(
             collective_id=0, has_side_effects=True, vmem_limit_bytes=56 * 1024 * 1024
@@ -607,7 +641,7 @@
             pltpu.VMEM((27, C, C), F32),
             pltpu.VMEM((1, C), F32),
             pltpu.VMEM((1, C), F32),
-            dma((5,)),
+            dma((7,)),
         ],
     )(*(pltpu.with_memory_space_constraint(v, pltpu.VMEM) for v in (raw, total, g2_raw)))
 

time: 62.7 us -> 63.5 us (1.013)
  Pallas kernels: 62 us -> 62.7 us
    pallas_call x1, Pallas kernels: 60.6 us -> 61.3 us  [local(): pl.pallas_call(kernel, out_shape=(pltpu.VMEM((C, NZ, NX, NY), BF16), pltp...]
where the time goes in v4:
time: 63.5 us; the launch traced here: 63.3 us
  Pallas kernels  62.7 us (99%)
  between operations  0.64 us (1%)
    pallas_call x1, Pallas kernels, local(): pl.pallas_call(kernel, out_shape=(pltpu.VMEM((C, NZ, NX, NY), BF16), pltp...  61.3 us
    pallas_call x1, Pallas kernels, local(): pl.pallas_call(results, out_shape=(jax.ShapeDtypeStruct((C, NZ, NX, NY),...  1.42 us

profile of v4, /device:TPU:1, one launch (start us, length us, event | category | flops | bytes accessed | tf_op | source)
XLA Modules:
  0.0 63.3 jit_solution(9671613863179021578)
XLA Ops:
  0.6 61.3 %shard_map.101 = (bf16[48,8,8,128]{3,2,1,0:T(8,128)(2,1)S(1)}, f32[2,512,128]{2,1,0:T(8,128)S(1)}, f32[27,48,48]{2,1,0:T(8,128)S(1)}) custom-call(bf16[48,8,8,128]{3,2,1,0:T(8,128)(2,1)} %bitcast.19, bf16[48,8,8,128]{3,2,1,0:T(8,128)(2,1)} %bitcast.20, bf16[27,48,48]{2,1,0:T(8,128)(2,1)} %bitcast.21, bf16[27,48,48]{2,1,0:T(8,128)(2,1)} %bitcast.22, ...), custom_call_target="tpu_custom_call" | custom-call | tf_op jit(solution)/shard_map/pallas_call | solution.py:571
  61.9 1.4 %shard_map.102 = (bf16[48,8,8,128]{3,2,1,0:T(8,128)(2,1)}, f32[27,48,48]{2,1,0:T(8,128)}, f32[27,48,48]{2,1,0:T(8,128)}, f32[1,48]{1,0:T(1,128)}, f32[1,48]{1,0:T(1,128)}) custom-call(bf16[48,8,8,128]{3,2,1,0:T(8,128)(2,1)S(1)} %get-tuple-element.13.raw, f32[2,512,128]{2,1,0:T(8,128)S(1)} %get-tuple-element.14.total, f32[27,48,48]{2,1,0:T(8,128)S(1)} %get-tuple-element.15.g2_raw), custom_call_target="tpu_custom_call" | custom-call | tf_op jit(solution)/shard_map/pallas_call | solution.py:629

commit v5 on v4

--- a/solution.py
+++ b/solution.py
@@ -260,8 +260,8 @@
     halo_start(*x_halo)
     loads[3].wait()
     unpack_own(g_ref, gim)
+    conv_inner(gim, w2f, gh)
     halo_start(*g_halo)
-    conv_inner(gim, w2f, gh)
 
     zero = jnp.zeros((C, NY), F32)
 
@@ -486,9 +486,15 @@
         acc[rows] += dot_nt(face, xim[(NZ + 1) * p, :, inner])
         pack(1, p, acc[pl.ds(pl.multiple_of((C // 2) * p, 8), SPLIT)], jnp.zeros((8, NY), F32))
 
-    grad_one(1 - core)
-    core_start(1)
-    grad_one(core)
+    def two_halves(h, carry):
+        grad_one(h * core + (1 - h) * (1 - core))
+
+        @pl.when(h == 0)
+        def _():
+            core_start(1)
+        return carry
+
+    lax.fori_loop(0, 2, two_halves, 0)
     core_finish(1)
 
     xy_finish(0)

time: 63.5 us -> 59 us (0.929)
  Pallas kernels: 62.7 us -> 58.2 us
    pallas_call x1, Pallas kernels: 61.3 us -> 56.8 us  [local(): pl.pallas_call(kernel, out_shape=(pltpu.VMEM((C, NZ, NX, NY), BF16), pltp...]
where the time goes in v5:
time: 59 us; the launch traced here: 58.9 us
  Pallas kernels  58.2 us (99%)
  between operations  0.64 us (1%)
    pallas_call x1, Pallas kernels, local(): pl.pallas_call(kernel, out_shape=(pltpu.VMEM((C, NZ, NX, NY), BF16), pltp...  56.8 us
    pallas_call x1, Pallas kernels, local(): pl.pallas_call(results, out_shape=(jax.ShapeDtypeStruct((C, NZ, NX, NY),...  1.42 us

profile of v5, /device:TPU:1, one launch (start us, length us, event | category | flops | bytes accessed | tf_op | source)
XLA Modules:
  0.0 58.9 jit_solution(12436878410813659499)
XLA Ops:
  0.6 56.8 %shard_map.101 = (bf16[48,8,8,128]{3,2,1,0:T(8,128)(2,1)S(1)}, f32[2,512,128]{2,1,0:T(8,128)S(1)}, f32[27,48,48]{2,1,0:T(8,128)S(1)}) custom-call(bf16[48,8,8,128]{3,2,1,0:T(8,128)(2,1)} %bitcast.19, bf16[48,8,8,128]{3,2,1,0:T(8,128)(2,1)} %bitcast.20, bf16[27,48,48]{2,1,0:T(8,128)(2,1)} %bitcast.21, bf16[27,48,48]{2,1,0:T(8,128)(2,1)} %bitcast.22, ...), custom_call_target="tpu_custom_call" | custom-call | tf_op jit(solution)/shard_map/pallas_call | solution.py:577
  57.5 1.4 %shard_map.102 = (bf16[48,8,8,128]{3,2,1,0:T(8,128)(2,1)}, f32[27,48,48]{2,1,0:T(8,128)}, f32[27,48,48]{2,1,0:T(8,128)}, f32[1,48]{1,0:T(1,128)}, f32[1,48]{1,0:T(1,128)}) custom-call(bf16[48,8,8,128]{3,2,1,0:T(8,128)(2,1)S(1)} %get-tuple-element.13.raw, f32[2,512,128]{2,1,0:T(8,128)S(1)} %get-tuple-element.14.total, f32[27,48,48]{2,1,0:T(8,128)S(1)} %get-tuple-element.15.g2_raw), custom_call_target="tpu_custom_call" | custom-call | tf_op jit(solution)/shard_map/pallas_call | solution.py:635

commit v6 on v5

--- a/solution.py
+++ b/solution.py
@@ -51,20 +51,11 @@
     me_z = z_hi * SZ_LO + z_lo
     sibling = (sp, dp + 1 - 2 * core)
 
-    def sp_dev(j):
-        return (j, dp)
-
     def xy_dev(j):
         return (z_hi * SY + j % SY, (j // SY) * (SZ_LO * 2) + z_lo * 2 + core)
 
     def z_dev(j):
         return ((j // SZ_LO) * SY + y, xx_ * (SZ_LO * 2) + (j % SZ_LO) * 2 + core)
-
-    def others(count, me, body):
-        def step(k, carry):
-            body(lax.rem(me + k, count))
-            return carry
-        lax.fori_loop(1, count, step, 0)
 
     ys = [(y + o) % SY for o in range(SY)]
     xs = [(xx_ + o) % SX for o in range(SX)]
@@ -227,15 +218,17 @@
 
     def st_copy(k, j, dev):
         return pltpu.make_async_remote_copy(
-            src_ref=st.at[k, sp], dst_ref=st.at[k, sp], send_sem=st_send.at[k, j],
-            recv_sem=st_recv.at[k, sp], device_id=dev, device_id_type=MESH,
-        )
-
-    def st_wait(k, j):
-        return pltpu.make_async_remote_copy(
-            src_ref=st.at[k, j], dst_ref=st.at[k, j], send_sem=st_send.at[k, j],
-            recv_sem=st_recv.at[k, j], device_id=sp_dev(j), device_id_type=MESH,
-        )
+            src_ref=st.at[k, sp], dst_ref=st.at[k, sp], send_sem=st_send.at[k],
+            recv_sem=st_recv.at[k], device_id=dev, device_id_type=MESH,
+        )
+
+    def bulk(ref, send, recv):
+        return pltpu.make_async_remote_copy(
+            src_ref=ref, dst_ref=ref, send_sem=send, recv_sem=recv, device_id=sibling, device_id_type=MESH,
+        )
+
+    def st_all(k):
+        return bulk(st.at[k, 0 : NSP - 1], st_send.at[k], st_recv.at[k])
 
     def st_start(k, one, two):
         row_one = as_row(jnp.sum(one, axis=1, keepdims=True))
@@ -248,7 +241,7 @@
         return mine
 
     def st_finish(k):
-        others(NSP, sp, lambda j: st_wait(k, j).wait_recv())
+        st_all(k).wait_recv()
         s = st[k, 0]
         for j in range(1, NSP):
             s = s + st[k, j]
@@ -333,14 +326,11 @@
     def xy_copy(k, j, dev):
         return pltpu.make_async_remote_copy(
             src_ref=half_sum.at[k, pl.ds(j * PIECE, PIECE)], dst_ref=xy_in.at[k, me_xy],
-            send_sem=xy_send.at[k, j], recv_sem=xy_recv.at[k, me_xy], device_id=dev, device_id_type=MESH,
-        )
-
-    def xy_wait(k, j):
-        return pltpu.make_async_remote_copy(
-            src_ref=xy_in.at[k, j], dst_ref=xy_in.at[k, j],
-            send_sem=xy_send.at[k, j], recv_sem=xy_recv.at[k, j], device_id=xy_dev(j), device_id_type=MESH,
-        )
+            send_sem=xy_send.at[k], recv_sem=xy_recv.at[k], device_id=dev, device_id_type=MESH,
+        )
+
+    def xy_all(k):
+        return bulk(xy_in.at[k, 0 : NXY - 1], xy_send.at[k], xy_recv.at[k])
 
     def core_finish(k):
         c_copy(k).wait_recv()
@@ -351,17 +341,14 @@
     def z_copy(k, j, dev):
         return pltpu.make_async_remote_copy(
             src_ref=z_in.at[k, me_z], dst_ref=z_in.at[k, me_z],
-            send_sem=z_send.at[k, j], recv_sem=z_recv.at[k, me_z], device_id=dev, device_id_type=MESH,
-        )
-
-    def z_wait(k, j):
-        return pltpu.make_async_remote_copy(
-            src_ref=z_in.at[k, j], dst_ref=z_in.at[k, j],
-            send_sem=z_send.at[k, j], recv_sem=z_recv.at[k, j], device_id=z_dev(j), device_id_type=MESH,
-        )
+            send_sem=z_send.at[k], recv_sem=z_recv.at[k], device_id=dev, device_id_type=MESH,
+        )
+
+    def z_all(k):
+        return bulk(z_in.at[k, 0 : NZZ - 1], z_send.at[k], z_recv.at[k])
 
     def xy_finish(k):
-        others(NXY, me_xy, lambda j: xy_wait(k, j).wait_recv())
+        xy_all(k).wait_recv()
         xy_in[k, me_xy] = half_sum[k, pl.ds(me_xy * PIECE, PIECE)]
         s = xy_in[k, 0]
         for j in range(1, NXY):
@@ -376,17 +363,17 @@
     def ga_copy(k, j, dev):
         return pltpu.make_async_remote_copy(
             src_ref=total.at[k, ga_at(me_xy)], dst_ref=total.at[k, ga_at(me_xy)],
-            send_sem=ga_send.at[k, j], recv_sem=ga_recv.at[k, me_xy], device_id=dev, device_id_type=MESH,
+            send_sem=ga_send.at[k], recv_sem=ga_recv.at[k, me_xy], device_id=dev, device_id_type=MESH,
         )
 
     def ga_wait(k, j):
         return pltpu.make_async_remote_copy(
             src_ref=total.at[k, ga_at(j)], dst_ref=total.at[k, ga_at(j)],
-            send_sem=ga_send.at[k, j], recv_sem=ga_recv.at[k, j], device_id=xy_dev(j), device_id_type=MESH,
+            send_sem=ga_send.at[k], recv_sem=ga_recv.at[k, j], device_id=xy_dev(j), device_id_type=MESH,
         )
 
     def z_finish(k):
-        others(NZZ, me_z, lambda j: z_wait(k, j).wait_recv())
+        z_all(k).wait_recv()
         s = z_in[k, 0]
         for j in range(1, NZZ):
             s = s + z_in[k, j]
@@ -399,7 +386,7 @@
         at = pl.ds(which * HALF + j * PIECE, PIECE)
         return pltpu.make_async_remote_copy(
             src_ref=total.at[k, at], dst_ref=total.at[k, at],
-            send_sem=cg_send.at[k, j], recv_sem=cg_recv.at[k, j], device_id=sibling, device_id_type=MESH,
+            send_sem=cg_send.at[k], recv_sem=cg_recv.at[k], device_id=sibling, device_id_type=MESH,
         )
 
     def gather_finish(k):
@@ -407,25 +394,20 @@
             ga_wait(k, j).wait_recv()
             cg_copy(k, core, j).start()
 
+    def cg_half(k, which):
+        return bulk(total.at[k, pl.ds(which * HALF, HALF)], cg_send.at[k], cg_recv.at[k])
+
+    def ga_sent(k):
+        bulk(total.at[k, 0 : HALF - PIECE], ga_send.at[k], ga_recv.at[k, 0]).wait_send()
+
     def drain(k):
-        others(NSP, sp, lambda j: st_copy(k, j, sp_dev(j)).wait_send())
-        others(NXY, me_xy, lambda j: xy_copy(k, j, xy_dev(j)).wait_send())
-        others(NXY, me_xy, lambda j: ga_copy(k, j, xy_dev(j)).wait_send())
-        others(NZZ, me_z, lambda j: z_copy(k, j, z_dev(j)).wait_send())
+        st_all(k).wait_send()
+        xy_all(k).wait_send()
+        z_all(k).wait_send()
         c_copy(k).wait_send()
-        all_sent(k)
 
     def all_finish(k):
-        def step(j, carry):
-            cg_copy(k, 1 - core, j).wait_recv()
-            return carry
-        lax.fori_loop(0, NXY, step, 0)
-
-    def all_sent(k):
-        def step(j, carry):
-            cg_copy(k, core, j).wait_send()
-            return carry
-        lax.fori_loop(0, NXY, step, 0)
+        cg_half(k, 1 - core).wait_recv()
 
     sides(him, 0, 0)
     lhs = jnp.concatenate(
@@ -497,11 +479,11 @@
     lax.fori_loop(0, 2, two_halves, 0)
     core_finish(1)
 
+    sides(pim, 1, NY)
     xy_finish(0)
-    sides(pim, 1, NY)
     conv_inner(pim, w1f, gh)
+    xy_finish(1)
     z_finish(0)
-    xy_finish(1)
     halo_wait(*p_halo)
 
     face_planes(hp, pim)
@@ -516,14 +498,18 @@
         return carry
 
     lax.fori_loop(1, NZ + 1, finish, 0)
+    z_finish(1)
     gather_finish(0)
-    z_finish(1)
     all_finish(0)
     separate(total, 0, g2_ref)
+    drain(0)
+    drain(1)
+    ga_sent(0)
+    cg_half(0, core).wait_send()
     gather_finish(1)
-    drain(0)
+    ga_sent(1)
     all_finish(1)
-    drain(1)
+    cg_half(1, core).wait_send()
 
 
 def separate(total, k, dst, done=None):
@@ -613,12 +599,12 @@
             pltpu.VMEM((2, NXY, PIECE, NY), F32),
             pltpu.VMEM((2, NZZ, PIECE, NY), F32),
             dma((3, 2)), dma((3, 2)),
-            dma((2, NSP)), dma((2, NSP)),
             dma((2,)), dma((2,)),
-            dma((2, NXY)), dma((2, NXY)),
-            dma((2, NZZ)), dma((2, NZZ)),
-            dma((2, NXY)), dma((2, NXY)),
-            dma((2, NXY)), dma((2, NXY)),
+            dma((2,)), dma((2,)),
+            dma((2,)), dma((2,)),
+            dma((2,)), dma((2,)),
+            dma((2,)), dma((2, NXY)),
+            dma((2,)), dma((2,)),
         ],
         compiler_params=pltpu.CompilerParams(
             collective_id=0, has_side_effects=True, vmem_limit_bytes=56 * 1024 * 1024

time: 59 us -> 55.1 us (0.934)
  Pallas kernels: 58.2 us -> 54.4 us
    pallas_call x1, Pallas kernels: 56.8 us -> 52.9 us  [local(): pl.pallas_call(kernel, out_shape=(pltpu.VMEM((C, NZ, NX, NY), BF16), pltp...]
where the time goes in v6:
time: 55.1 us; the launch traced here: 55 us
  Pallas kernels  54.4 us (99%)
  between operations  0.64 us (1%)
    pallas_call x1, Pallas kernels, local(): pl.pallas_call(kernel, out_shape=(pltpu.VMEM((C, NZ, NX, NY), BF16), pltp...  52.9 us
    pallas_call x1, Pallas kernels, local(): pl.pallas_call(results, out_shape=(jax.ShapeDtypeStruct((C, NZ, NX, NY),...  1.42 us

profile of v6, /device:TPU:1, one launch (start us, length us, event | category | flops | bytes accessed | tf_op | source)
XLA Modules:
  0.0 55.0 jit_solution(2339291792061890989)
XLA Ops:
  0.6 52.9 %shard_map.101 = (bf16[48,8,8,128]{3,2,1,0:T(8,128)(2,1)S(1)}, f32[2,512,128]{2,1,0:T(8,128)S(1)}, f32[27,48,48]{2,1,0:T(8,128)S(1)}) custom-call(bf16[48,8,8,128]{3,2,1,0:T(8,128)(2,1)} %bitcast.19, bf16[48,8,8,128]{3,2,1,0:T(8,128)(2,1)} %bitcast.20, bf16[27,48,48]{2,1,0:T(8,128)(2,1)} %bitcast.21, bf16[27,48,48]{2,1,0:T(8,128)(2,1)} %bitcast.22, ...), custom_call_target="tpu_custom_call" | custom-call | tf_op jit(solution)/shard_map/pallas_call | solution.py:563
  53.6 1.4 %shard_map.102 = (bf16[48,8,8,128]{3,2,1,0:T(8,128)(2,1)}, f32[27,48,48]{2,1,0:T(8,128)}, f32[27,48,48]{2,1,0:T(8,128)}, f32[1,48]{1,0:T(1,128)}, f32[1,48]{1,0:T(1,128)}) custom-call(bf16[48,8,8,128]{3,2,1,0:T(8,128)(2,1)S(1)} %get-tuple-element.13.raw, f32[2,512,128]{2,1,0:T(8,128)S(1)} %get-tuple-element.14.total, f32[27,48,48]{2,1,0:T(8,128)S(1)} %get-tuple-element.15.g2_raw), custom_call_target="tpu_custom_call" | custom-call | tf_op jit(solution)/shard_map/pallas_call | solution.py:621

commit v7 on v6

--- a/solution.py
+++ b/solution.py
@@ -73,6 +73,14 @@
     z_ids = [(me_z + o) % NZZ for o in (4, 3, 5, 2, 6, 1, 7)]
     z_peers = [(j, z_dev(j)) for j in z_ids]
 
+    barrier = pltpu.get_barrier_semaphore()
+
+    def greet(dev):
+        pl.semaphore_signal(barrier, inc=1, device_id=dev, device_id_type=MESH)
+
+    for _, dev in sp_peers:
+        greet(dev)
+
     loads = [
         pltpu.make_async_copy(src, dst, load.at[i])
         for i, (src, dst) in enumerate(
@@ -82,12 +90,7 @@
     for each in loads:
         each.start()
 
-    barrier = pltpu.get_barrier_semaphore()
-
-    def greet(dev):
-        pl.semaphore_signal(barrier, inc=1, device_id=dev, device_id_type=MESH)
-
-    for _, dev in sp_peers + z_peers + xy_peers:
+    for _, dev in z_peers + xy_peers:
         greet(dev)
     greet(sibling)
 
@@ -363,13 +366,7 @@
     def ga_copy(k, j, dev):
         return pltpu.make_async_remote_copy(
             src_ref=total.at[k, ga_at(me_xy)], dst_ref=total.at[k, ga_at(me_xy)],
-            send_sem=ga_send.at[k], recv_sem=ga_recv.at[k, me_xy], device_id=dev, device_id_type=MESH,
-        )
-
-    def ga_wait(k, j):
-        return pltpu.make_async_remote_copy(
-            src_ref=total.at[k, ga_at(j)], dst_ref=total.at[k, ga_at(j)],
-            send_sem=ga_send.at[k], recv_sem=ga_recv.at[k, j], device_id=xy_dev(j), device_id_type=MESH,
+            send_sem=ga_send.at[k], recv_sem=ga_recv.at[k], device_id=dev, device_id_type=MESH,
         )
 
     def z_finish(k):
@@ -378,27 +375,18 @@
         for j in range(1, NZZ):
             s = s + z_in[k, j]
         total[k, ga_at(me_xy)] = s
-        cg_copy(k, core, me_xy).start()
         for j, dev in xy_peers:
             ga_copy(k, j, dev).start()
 
-    def cg_copy(k, which, j):
-        at = pl.ds(which * HALF + j * PIECE, PIECE)
-        return pltpu.make_async_remote_copy(
-            src_ref=total.at[k, at], dst_ref=total.at[k, at],
-            send_sem=cg_send.at[k], recv_sem=cg_recv.at[k], device_id=sibling, device_id_type=MESH,
-        )
-
     def gather_finish(k):
-        for j, _ in reversed(xy_peers):
-            ga_wait(k, j).wait_recv()
-            cg_copy(k, core, j).start()
+        bulk(total.at[k, 0 : HALF - PIECE], ga_send.at[k], ga_recv.at[k]).wait_recv()
+        cg_half(k, core).start()
 
     def cg_half(k, which):
         return bulk(total.at[k, pl.ds(which * HALF, HALF)], cg_send.at[k], cg_recv.at[k])
 
     def ga_sent(k):
-        bulk(total.at[k, 0 : HALF - PIECE], ga_send.at[k], ga_recv.at[k, 0]).wait_send()
+        bulk(total.at[k, 0 : HALF - PIECE], ga_send.at[k], ga_recv.at[k]).wait_send()
 
     def drain(k):
         st_all(k).wait_send()
@@ -479,8 +467,8 @@
     lax.fori_loop(0, 2, two_halves, 0)
     core_finish(1)
 
+    xy_finish(0)
     sides(pim, 1, NY)
-    xy_finish(0)
     conv_inner(pim, w1f, gh)
     xy_finish(1)
     z_finish(0)
@@ -603,7 +591,7 @@
             dma((2,)), dma((2,)),
             dma((2,)), dma((2,)),
             dma((2,)), dma((2,)),
-            dma((2,)), dma((2, NXY)),
+            dma((2,)), dma((2,)),
             dma((2,)), dma((2,)),
         ],
         compiler_params=pltpu.CompilerParams(

time: 55.1 us -> 55 us (level)
  no operation moved by 1% of the time
where the time goes in v7:
time: 55 us; the launch traced here: 54.9 us
  Pallas kernels  54.3 us (99%)
  between operations  0.64 us (1%)
    pallas_call x1, Pallas kernels, local(): pl.pallas_call(kernel, out_shape=(pltpu.VMEM((C, NZ, NX, NY), BF16), pltp...  52.9 us
    pallas_call x1, Pallas kernels, local(): pl.pallas_call(results, out_shape=(jax.ShapeDtypeStruct((C, NZ, NX, NY),...  1.42 us

profile of v7, /device:TPU:1, one launch (start us, length us, event | category | flops | bytes accessed | tf_op | source)
XLA Modules:
  0.0 54.9 jit_solution(13874441432906545671)
XLA Ops:
  0.6 52.9 %shard_map.101 = (bf16[48,8,8,128]{3,2,1,0:T(8,128)(2,1)S(1)}, f32[2,512,128]{2,1,0:T(8,128)S(1)}, f32[27,48,48]{2,1,0:T(8,128)S(1)}) custom-call(bf16[48,8,8,128]{3,2,1,0:T(8,128)(2,1)} %bitcast.19, bf16[48,8,8,128]{3,2,1,0:T(8,128)(2,1)} %bitcast.20, bf16[27,48,48]{2,1,0:T(8,128)(2,1)} %bitcast.21, bf16[27,48,48]{2,1,0:T(8,128)(2,1)} %bitcast.22, ...), custom_call_target="tpu_custom_call" | custom-call | tf_op jit(solution)/shard_map/pallas_call | solution.py:551
  53.5 1.4 %shard_map.102 = (bf16[48,8,8,128]{3,2,1,0:T(8,128)(2,1)}, f32[27,48,48]{2,1,0:T(8,128)}, f32[27,48,48]{2,1,0:T(8,128)}, f32[1,48]{1,0:T(1,128)}, f32[1,48]{1,0:T(1,128)}) custom-call(bf16[48,8,8,128]{3,2,1,0:T(8,128)(2,1)S(1)} %get-tuple-element.13.raw, f32[2,512,128]{2,1,0:T(8,128)S(1)} %get-tuple-element.14.total, f32[27,48,48]{2,1,0:T(8,128)S(1)} %get-tuple-element.15.g2_raw), custom_call_target="tpu_custom_call" | custom-call | tf_op jit(solution)/shard_map/pallas_call | solution.py:609
